TPU v7x, 32 devices: a whole 2x2x4 slice. The times are simulated.
32 devices in a mesh: blk: 16 (over z, y, core), head: 2 (over x).
Axes of the slice: x: 2, y: 2, z: 4, core: 2. Of those that a mesh axis runs over, the one named last changes fastest.
Arguments:
- queries: bfloat16 [3072, 4096], P(('blk', 'head'))
- key_rows: bfloat16 [3072, 1024], P(('blk', 'head'))
- value_rows: bfloat16 [3072, 1024], P(('blk', 'head')), may hold values from -6 to 6
- visit_ids: int32 [3072], replicated, may hold values from 0 to 3, as said below
- span_order: int32 [16], replicated, may hold values from 0 to 15, each once
Outputs:
- attended: bfloat16 [3072, 4096], P(('blk', 'head'))
Inputs may be any that keep to these rules, and one draw needn't show every extreme that they name: `visit_ids`: visit ids never fall along time; every one of the 4 visits has events and begins at an even position. `span_order`: each block index holds a different block of 192 consecutive events.
All inputs are finite; a program needn't handle non-finite values.
Results may differ from a plain program's by a relative error of at most 0.0049.
Values may be sent and summed in bfloat16 or wider, within the bound.
A program may use at most 64 MiB of HBM per device.

v0:
```python
import jax
import jax.numpy as jnp
from jax import lax
from jax.sharding import PartitionSpec as P

HEADS = 32
KV_HEADS = 8
HEAD_DIM = 128


masked_score = -1e30


def span_of(cycle_positions, span_order):
    table_index = jnp.arange(span_order.shape[0], dtype=jnp.int32)
    picked = jnp.where(cycle_positions[:, None] == table_index[None, :], span_order[None, :], 0)
    return jnp.sum(picked, axis=1)


def body(queries, key_rows, value_rows, visit_ids, span_order):
    head_queries, head_keys, head_values = (
        lax.all_to_all(queries, "head", split_axis=1, concat_axis=0, tiled=True),
        lax.all_to_all(key_rows, "head", split_axis=1, concat_axis=0, tiled=True),
        lax.all_to_all(value_rows, "head", split_axis=1, concat_axis=0, tiled=True),
    )
    row_count = head_queries.shape[0]
    group_size = HEADS // KV_HEADS
    local_heads = head_keys.shape[1] // HEAD_DIM
    grouped = head_queries.reshape(row_count, local_heads, group_size, HEAD_DIM)
    cycle_index = lax.axis_index("blk")
    score_scale = HEAD_DIM ** (-0.5)
    my_span = span_of(jnp.full((1,), cycle_index, jnp.int32), span_order)[0]
    query_pos = my_span * row_count + jnp.arange(row_count, dtype=jnp.int32)
    query_visit = jnp.take(visit_ids, query_pos)

    def attend(state_now, kv_block, first_row):
        width = kv_block.shape[1]
        global_rows = first_row + jnp.arange(width, dtype=jnp.int32)
        key_pos = (
            span_of(global_rows // row_count, span_order) * row_count + global_rows % row_count
        )
        key_visit = jnp.take(visit_ids, key_pos)
        allowed = (key_pos[None, :] <= query_pos[:, None]) & (
            key_visit[None, :] == query_visit[:, None]
        )
        run_max, run_total, run_acc = state_now
        key_heads = kv_block[0].reshape(width, local_heads, HEAD_DIM)
        value_heads = kv_block[1].reshape(width, local_heads, HEAD_DIM)
        scores = (
            jnp.einsum("qhgd,khd->qhgk", grouped, key_heads, preferred_element_type=jnp.float32)
            * score_scale
        )
        mask_wide = allowed[:, None, None, :]
        masked = jnp.where(mask_wide, scores, masked_score)
        new_max = jnp.maximum(run_max, jnp.max(masked, axis=-1))
        factor = jnp.exp(run_max - new_max)
        weights = jnp.where(mask_wide, jnp.exp(masked - new_max[..., None]), 0.0)
        new_total = run_total * factor + jnp.sum(weights, axis=-1)
        new_acc = run_acc * factor[..., None] + jnp.einsum(
            "qhgk,khd->qhgd",
            weights.astype(jnp.bfloat16),
            value_heads,
            preferred_element_type=jnp.float32,
        )
        return (new_max, new_total, new_acc)

    kv_local = jnp.stack([head_keys, head_values])
    stat_shape = (row_count, local_heads, group_size)
    initial = (
        jnp.full(stat_shape, masked_score, jnp.float32),
        jnp.zeros(stat_shape, jnp.float32),
        jnp.zeros(stat_shape + (HEAD_DIM,), jnp.float32),
    )
    part_rows = lax.all_gather(kv_local, "blk", axis=1, tiled=True)
    width = part_rows.shape[1]
    step_rows = width
    step_rows = 4 * row_count

    def inner(turn_index, state_in):
        offset = turn_index * step_rows
        sub_block = lax.dynamic_slice_in_dim(part_rows, offset, step_rows, 1)
        return attend(state_in, sub_block, offset)

    state_now = lax.fori_loop(0, width // step_rows, inner, initial)
    run_max, run_total, run_acc = state_now
    attended_local = (run_acc / run_total[..., None]).astype(jnp.bfloat16)
    attended_local = attended_local.reshape(row_count, local_heads * group_size * HEAD_DIM)
    return lax.all_to_all(attended_local, "head", split_axis=0, concat_axis=1, tiled=True)


def solution(mesh):
    placed = (
        P(("blk", "head"), None),
        P(("blk", "head"), None),
        P(("blk", "head"), None),
        P(),
        P(),
    )
    return jax.shard_map(
        body, mesh=mesh, in_specs=placed, out_specs=P(("blk", "head"), None), check_vma=False
    )
```

profile of v0, /device:TPU:0, one launch (start us, length us, event | category | flops | bytes accessed | tf_op | source)
XLA Modules:
  0.0 179.4 jit_solution(12708668806234442807)
XLA Ops:
  6.5 1.6 copy.67
  8.2 4.2 %all-to-all-start = ((bf16[96,2,512]{2,0,1:T(8,128)(2,1)}), bf16[96,2,512]{2,0,1:T(8,128)(2,1)S(1)}, u32[]{:S(2)}, u32[]{:S(2)}) async-start(bf16[96,2,512]{2,0,1:T(8,128)(2,1)} %bitcast.50), calls=%async_computation | async-start | bytes 393216 | tf_op jit(solution)/shard_map/all_to_all | solution.py:23
  12.4 0.9 copy.66
  13.3 4.2 %all-to-all-done = bf16[96,2,512]{2,0,1:T(8,128)(2,1)S(1)} async-done(((bf16[96,2,512]{2,0,1:T(8,128)(2,1)}), bf16[96,2,512]{2,0,1:T(8,128)(2,1)S(1)}, u32[]{:S(2)}, u32[]{:S(2)}) %all-to-all-start) | async-done | bytes 196640 | tf_op jit(solution)/shard_map/all_to_all | solution.py:23
  17.5 7.2 %all_to_all.67 = bf16[96,2,512]{2,0,1:T(8,128)(2,1)S(1)} all-to-all(bf16[96,2,512]{2,0,1:T(8,128)(2,1)S(1)} %bitcast.74), channel_id=1, replica_groups=mesh['blk'=16,'head'=2] {'head'}, dimensions={1} | all-to-all | bytes 393216 | tf_op jit(solution)/shard_map/all_to_all | solution.py:24
  24.7 0.8 pad_maximum_fusion
  25.5 2.1 %copy.65 = bf16[12,2,8,2048]{3,2,0,1:T(8,128)(2,1)} copy(bf16[12,2,8,2048]{3,2,1,0:T(8,128)(2,1)} %bitcast.73) | data formatting | bytes 1572864 | tf_op jit(solution)/shard_map/all_to_all | solution.py:22
  27.6 3.5 %all-to-all-start.2 = ((bf16[96,2,2048]{2,0,1:T(8,128)(2,1)}), bf16[96,2,2048]{2,0,1:T(8,128)(2,1)S(1)}, u32[]{:S(2)}, u32[]{:S(2)}) async-start(bf16[96,2,2048]{2,0,1:T(8,128)(2,1)} %bitcast.48), calls=%async_computation.2 | async-start | bytes 1572864 | tf_op jit(solution)/shard_map/all_to_all | solution.py:22
  31.2 1.3 fusion.22
  33.2 2.0 %gather_fusion.1 = s32[192]{0:T(256)S(1)} fusion(s32[3072]{0:T(1024)} %param.10, s32[1024]{0:T(1024)S(1)} %pad_clamp_fusion.1), kind=kCustom, calls=%fused_computation.1 | custom fusion | bytes 2304 | tf_op jit(solution)/shard_map/jit(_take)/gather | solution.py:34
  35.2 5.4 %all-to-all-done.2 = bf16[96,2,2048]{2,0,1:T(8,128)(2,1)S(1)} async-done(((bf16[96,2,2048]{2,0,1:T(8,128)(2,1)}), bf16[96,2,2048]{2,0,1:T(8,128)(2,1)S(1)}, u32[]{:S(2)}, u32[]{:S(2)}) %all-to-all-start.2) | async-done | bytes 786464 | tf_op jit(solution)/shard_map/all_to_all | solution.py:22
  40.5 0.6 reshape.209
  41.3 47.0 %all-gather.2.cloned.1.call-done = bf16[2,3072,512]{2,1,0:T(8,128)(2,1)} async-done(((bf16[2,192,512]{2,1,0:T(8,128)(2,1)}), bf16[2,3072,512]{2,1,0:T(8,128)(2,1)}) %all-gather.2.cloned.1.call-update) | async-done | bytes 6291472 | tf_op jit(solution)/shard_map/all_gather | solution.py:74
  88.3 66.2 %while.20 = (s32[]{:T(128)}, f32[192,4,4]{0,2,1:T(4,128)S(1)}, f32[192,4,4]{0,2,1:T(4,128)S(1)}, f32[192,4,4,128]{3,0,2,1:T(8,128)}, s32[16]{0:T(128)S(1)}, /*in...) while((s32[]{:T(128)}, f32[192,4,4]{0,2,1:T(4,128)S(1)}, ...), condition=%wide.region_5.6_spmd.clone, body=%wide.region_1.5_spmd.clone.sunk | while | flops 1240333568 | bytes 53536360 | solution.py:84
  88.5 4.5 %gather_fusion = s32[768]{0:T(1024)S(1)} fusion(s32[3072]{0:T(1024)S(1)} %get-tuple-element.479, s32[1024]{0:T(1024)S(1)} %pad_clamp_fusion.3), kind=kCustom, calls=%fused_computation.clone.clone.1 | custom fusion | bytes 9216 | tf_op jit(solution)/shard_map/while/body/eval_jaxpr/jit(_take)/gather | solution.py:42
  93.2 1.5 constant_dynamic-slice_fusion.3
  94.7 0.3 copy.70
  94.9 0.3 copy.71
  95.2 2.0 %fusion.40 = (f32[192,4,4]{0,2,1:T(4,128)S(1)}, f32[4,768,192,4]{1,2,3,0:T(8,128)S(1)}) fusion(pred[192,768]{1,0:T(8,128)(4,1)S(1)} %compare_and_fusion.2, bf16[768,4,128,1]{0,2,3,1:T(8,128)(2,1)S(1)} %bitcast.69, bf16[192,4,4,128]{3,0,2,1:T(8,128)(2,1)S(1)} %get-tuple-element.482), kind=kOutput, calls=%fused_computation.5.clone.1 | convolution fusion | flops 611054592 | bytes 11169792 | tf_op jit(solution)/shard_map/while/body/eval_jaxpr/qhgd,khd->qhgk/dot_general | solution.py:50
  97.2 3.1 %fusion.41 = f32[192,4,4]{0,2,1:T(4,128)S(1)} fusion(f32[4,768,192,4]{1,2,3,0:T(8,128)S(1)} %get-tuple-element.440, f32[192,4,4]{0,2,1:T(4,128)S(1)} %select_maximum_fusion.2, pred[192,768]{1,0:T(8,128)(4,1)S(1)} %compare_and_fusion.2), kind=kLoop, calls=%fused_computation.7.clone.1 | loop fusion | flops 11793408 | bytes 9609216 | tf_op jit(solution)/shard_map/while/body/eval_jaxpr/reduce_sum | solution.py:58
  100.3 3.4 %bitcast_add_fusion.2 = f32[192,4,4,128]{3,0,2,1:T(8,128)S(1)} fusion(f32[192,4,4,128]{3,0,2,1:T(8,128)S(1)} %copy-done.1, bf16[768,4,128,1]{0,2,3,1:T(8,128)(2,1)S(1)} %bitcast.70, f32[4,768,192,4]{1,2,3,0:T(8,128)S(1)} %get-tuple-element.440, f32[192,4,4]{0,2,1:T(4,128)S(1)} %select_maximum_fusion.2, pred[192,768]{1,0:T(8,128)(4,1)S(1)} %compare_and_fusion.2, ...), kind=kOutput, calls=%fused_computation.10.clone.1 | convolution fusion | flops 616955904 | bytes 13541377 | tf_op jit(solution)/shard_map/while/body/eval_jaxpr/qhgk,khd->qhgd/dot_general | solution.py:59
  103.7 1.1 copy-done.2
  105.0 4.5 %gather_fusion = s32[768]{0:T(1024)S(1)} fusion(s32[3072]{0:T(1024)S(1)} %get-tuple-element.479, s32[1024]{0:T(1024)S(1)} %pad_clamp_fusion.3), kind=kCustom, calls=%fused_computation.clone.clone.1 | custom fusion | bytes 9216 | tf_op jit(solution)/shard_map/while/body/eval_jaxpr/jit(_take)/gather | solution.py:42
  109.7 1.5 constant_dynamic-slice_fusion.3
  111.2 0.3 copy.70
  111.8 2.0 %fusion.40 = (f32[192,4,4]{0,2,1:T(4,128)S(1)}, f32[4,768,192,4]{1,2,3,0:T(8,128)S(1)}) fusion(pred[192,768]{1,0:T(8,128)(4,1)S(1)} %compare_and_fusion.2, bf16[768,4,128,1]{0,2,3,1:T(8,128)(2,1)S(1)} %bitcast.69, bf16[192,4,4,128]{3,0,2,1:T(8,128)(2,1)S(1)} %get-tuple-element.482), kind=kOutput, calls=%fused_computation.5.clone.1 | convolution fusion | flops 611054592 | bytes 11169792 | tf_op jit(solution)/shard_map/while/body/eval_jaxpr/qhgd,khd->qhgk/dot_general | solution.py:50
  113.7 3.1 %fusion.41 = f32[192,4,4]{0,2,1:T(4,128)S(1)} fusion(f32[4,768,192,4]{1,2,3,0:T(8,128)S(1)} %get-tuple-element.440, f32[192,4,4]{0,2,1:T(4,128)S(1)} %select_maximum_fusion.2, pred[192,768]{1,0:T(8,128)(4,1)S(1)} %compare_and_fusion.2), kind=kLoop, calls=%fused_computation.7.clone.1 | loop fusion | flops 11793408 | bytes 9609216 | tf_op jit(solution)/shard_map/while/body/eval_jaxpr/reduce_sum | solution.py:58
  116.9 3.4 %bitcast_add_fusion.2 = f32[192,4,4,128]{3,0,2,1:T(8,128)S(1)} fusion(f32[192,4,4,128]{3,0,2,1:T(8,128)S(1)} %copy-done.1, bf16[768,4,128,1]{0,2,3,1:T(8,128)(2,1)S(1)} %bitcast.70, f32[4,768,192,4]{1,2,3,0:T(8,128)S(1)} %get-tuple-element.440, f32[192,4,4]{0,2,1:T(4,128)S(1)} %select_maximum_fusion.2, pred[192,768]{1,0:T(8,128)(4,1)S(1)} %compare_and_fusion.2, ...), kind=kOutput, calls=%fused_computation.10.clone.1 | convolution fusion | flops 616955904 | bytes 13541377 | tf_op jit(solution)/shard_map/while/body/eval_jaxpr/qhgk,khd->qhgd/dot_general | solution.py:59
  120.3 1.1 copy-done.2
  121.6 4.5 %gather_fusion = s32[768]{0:T(1024)S(1)} fusion(s32[3072]{0:T(1024)S(1)} %get-tuple-element.479, s32[1024]{0:T(1024)S(1)} %pad_clamp_fusion.3), kind=kCustom, calls=%fused_computation.clone.clone.1 | custom fusion | bytes 9216 | tf_op jit(solution)/shard_map/while/body/eval_jaxpr/jit(_take)/gather | solution.py:42
  126.3 1.5 constant_dynamic-slice_fusion.3
  128.0 0.3 copy.71
  128.3 2.0 %fusion.40 = (f32[192,4,4]{0,2,1:T(4,128)S(1)}, f32[4,768,192,4]{1,2,3,0:T(8,128)S(1)}) fusion(pred[192,768]{1,0:T(8,128)(4,1)S(1)} %compare_and_fusion.2, bf16[768,4,128,1]{0,2,3,1:T(8,128)(2,1)S(1)} %bitcast.69, bf16[192,4,4,128]{3,0,2,1:T(8,128)(2,1)S(1)} %get-tuple-element.482), kind=kOutput, calls=%fused_computation.5.clone.1 | convolution fusion | flops 611054592 | bytes 11169792 | tf_op jit(solution)/shard_map/while/body/eval_jaxpr/qhgd,khd->qhgk/dot_general | solution.py:50
  130.3 3.1 %fusion.41 = f32[192,4,4]{0,2,1:T(4,128)S(1)} fusion(f32[4,768,192,4]{1,2,3,0:T(8,128)S(1)} %get-tuple-element.440, f32[192,4,4]{0,2,1:T(4,128)S(1)} %select_maximum_fusion.2, pred[192,768]{1,0:T(8,128)(4,1)S(1)} %compare_and_fusion.2), kind=kLoop, calls=%fused_computation.7.clone.1 | loop fusion | flops 11793408 | bytes 9609216 | tf_op jit(solution)/shard_map/while/body/eval_jaxpr/reduce_sum | solution.py:58
  133.4 3.4 %bitcast_add_fusion.2 = f32[192,4,4,128]{3,0,2,1:T(8,128)S(1)} fusion(f32[192,4,4,128]{3,0,2,1:T(8,128)S(1)} %copy-done.1, bf16[768,4,128,1]{0,2,3,1:T(8,128)(2,1)S(1)} %bitcast.70, f32[4,768,192,4]{1,2,3,0:T(8,128)S(1)} %get-tuple-element.440, f32[192,4,4]{0,2,1:T(4,128)S(1)} %select_maximum_fusion.2, pred[192,768]{1,0:T(8,128)(4,1)S(1)} %compare_and_fusion.2, ...), kind=kOutput, calls=%fused_computation.10.clone.1 | convolution fusion | flops 616955904 | bytes 13541377 | tf_op jit(solution)/shard_map/while/body/eval_jaxpr/qhgk,khd->qhgd/dot_general | solution.py:59
  136.8 1.1 copy-done.2
  138.1 4.5 %gather_fusion = s32[768]{0:T(1024)S(1)} fusion(s32[3072]{0:T(1024)S(1)} %get-tuple-element.479, s32[1024]{0:T(1024)S(1)} %pad_clamp_fusion.3), kind=kCustom, calls=%fused_computation.clone.clone.1 | custom fusion | bytes 9216 | tf_op jit(solution)/shard_map/while/body/eval_jaxpr/jit(_take)/gather | solution.py:42
  142.8 1.5 constant_dynamic-slice_fusion.3
  144.3 0.3 copy.70
  144.9 2.0 %fusion.40 = (f32[192,4,4]{0,2,1:T(4,128)S(1)}, f32[4,768,192,4]{1,2,3,0:T(8,128)S(1)}) fusion(pred[192,768]{1,0:T(8,128)(4,1)S(1)} %compare_and_fusion.2, bf16[768,4,128,1]{0,2,3,1:T(8,128)(2,1)S(1)} %bitcast.69, bf16[192,4,4,128]{3,0,2,1:T(8,128)(2,1)S(1)} %get-tuple-element.482), kind=kOutput, calls=%fused_computation.5.clone.1 | convolution fusion | flops 611054592 | bytes 11169792 | tf_op jit(solution)/shard_map/while/body/eval_jaxpr/qhgd,khd->qhgk/dot_general | solution.py:50
  146.9 3.1 %fusion.41 = f32[192,4,4]{0,2,1:T(4,128)S(1)} fusion(f32[4,768,192,4]{1,2,3,0:T(8,128)S(1)} %get-tuple-element.440, f32[192,4,4]{0,2,1:T(4,128)S(1)} %select_maximum_fusion.2, pred[192,768]{1,0:T(8,128)(4,1)S(1)} %compare_and_fusion.2), kind=kLoop, calls=%fused_computation.7.clone.1 | loop fusion | flops 11793408 | bytes 9609216 | tf_op jit(solution)/shard_map/while/body/eval_jaxpr/reduce_sum | solution.py:58
  150.0 3.4 %bitcast_add_fusion.2 = f32[192,4,4,128]{3,0,2,1:T(8,128)S(1)} fusion(f32[192,4,4,128]{3,0,2,1:T(8,128)S(1)} %copy-done.1, bf16[768,4,128,1]{0,2,3,1:T(8,128)(2,1)S(1)} %bitcast.70, f32[4,768,192,4]{1,2,3,0:T(8,128)S(1)} %get-tuple-element.440, f32[192,4,4]{0,2,1:T(4,128)S(1)} %select_maximum_fusion.2, pred[192,768]{1,0:T(8,128)(4,1)S(1)} %compare_and_fusion.2, ...), kind=kOutput, calls=%fused_computation.10.clone.1 | convolution fusion | flops 616955904 | bytes 13541377 | tf_op jit(solution)/shard_map/while/body/eval_jaxpr/qhgk,khd->qhgd/dot_general | solution.py:59
  153.4 1.1 copy-done.2
  154.5 1.9 %divide_convert_fusion = bf16[192,4,4,128]{3,0,2,1:T(8,128)(2,1)S(1)} fusion(f32[192,4,4,128]{3,0,2,1:T(8,128)} %get-tuple-element.251, f32[192,4,4]{0,2,1:T(4,128)S(1)} %get-tuple-element.252), kind=kLoop, calls=%fused_computation.43 | loop fusion | flops 786432 | bytes 2371584 | tf_op jit(solution)/shard_map/convert_element_type | solution.py:86
  156.4 0.6 copy.47
  157.0 0.6 all_to_all.59
  157.6 13.9 %all_to_all.68 = bf16[2,96,2048]{2,1,0:T(8,128)(2,1)S(1)} all-to-all(bf16[2,96,2048]{2,1,0:T(8,128)(2,1)S(1)} %all_to_all.59), channel_id=1, replica_groups=mesh['blk'=16,'head'=2] {'head'}, dimensions={0} | all-to-all | bytes 1572864 | tf_op jit(solution)/shard_map/all_to_all | solution.py:88
  171.6 1.0 copy.61
  (72 shorter events, 2.7 us)
Async XLA Ops:
  6.5 81.8 %copy-start.3 = (s32[16]{0:T(128)S(1)}, s32[16]{0:T(128)}, u32[]{:S(2)}) copy-start(s32[16]{0:T(128)} %param.11) | copy-start | bytes 196
  6.5 81.8 %copy-start = (s32[3072]{0:T(1024)S(1)}, s32[3072]{0:T(1024)}, u32[]{:S(2)}) copy-start(s32[3072]{0:T(1024)} %param.10) | copy-start | bytes 36868
  8.2 9.4 %all-to-all-start = ((bf16[96,2,512]{2,0,1:T(8,128)(2,1)}), bf16[96,2,512]{2,0,1:T(8,128)(2,1)S(1)}, u32[]{:S(2)}, u32[]{:S(2)}) async-start(bf16[96,2,512]{2,0,1:T(8,128)(2,1)} %bitcast.50), calls=%async_computation | async-start | bytes 393216 | tf_op jit(solution)/shard_map/all_to_all | solution.py:23
  12.4 75.9 %all-gather.2.cloned.1.call-start = ((), (), s32[]{:S(2)}) async-start(), calls=%async_computation.4 | async-start | bytes 6684672 | tf_op jit(solution)/shard_map/all_gather | solution.py:74
  27.6 12.9 %all-to-all-start.2 = ((bf16[96,2,2048]{2,0,1:T(8,128)(2,1)}), bf16[96,2,2048]{2,0,1:T(8,128)(2,1)S(1)}, u32[]{:S(2)}, u32[]{:S(2)}) async-start(bf16[96,2,2048]{2,0,1:T(8,128)(2,1)} %bitcast.48), calls=%async_computation.2 | async-start | bytes 1572864 | tf_op jit(solution)/shard_map/all_to_all | solution.py:22
  95.2 5.1 %copy-start.1 = (f32[192,4,4,128]{3,0,2,1:T(8,128)S(1)}, f32[192,4,4,128]{3,0,2,1:T(8,128)}, u32[]{:S(2)}) copy-start(f32[192,4,4,128]{3,0,2,1:T(8,128)} %get-tuple-element.462) | copy-start | bytes 4718596 | tf_op jit(solution)/shard_map/while
  103.7 1.2 copy-start.2
  111.8 5.1 %copy-start.1 = (f32[192,4,4,128]{3,0,2,1:T(8,128)S(1)}, f32[192,4,4,128]{3,0,2,1:T(8,128)}, u32[]{:S(2)}) copy-start(f32[192,4,4,128]{3,0,2,1:T(8,128)} %get-tuple-element.462) | copy-start | bytes 4718596 | tf_op jit(solution)/shard_map/while
  120.3 1.2 copy-start.2
  128.3 5.1 %copy-start.1 = (f32[192,4,4,128]{3,0,2,1:T(8,128)S(1)}, f32[192,4,4,128]{3,0,2,1:T(8,128)}, u32[]{:S(2)}) copy-start(f32[192,4,4,128]{3,0,2,1:T(8,128)} %get-tuple-element.462) | copy-start | bytes 4718596 | tf_op jit(solution)/shard_map/while
  136.8 1.2 copy-start.2
  144.9 5.1 %copy-start.1 = (f32[192,4,4,128]{3,0,2,1:T(8,128)S(1)}, f32[192,4,4,128]{3,0,2,1:T(8,128)}, u32[]{:S(2)}) copy-start(f32[192,4,4,128]{3,0,2,1:T(8,128)} %get-tuple-element.462) | copy-start | bytes 4718596 | tf_op jit(solution)/shard_map/while
  153.4 1.2 copy-start.2
Sparse Core Ops, SparseCore 0:
  25.7 62.5 all-gather.1
where the time goes:
time: 180 us; the launch traced here: 179 us
  waiting for transfers between devices  56.6 us (31%)
  local copies, waits for them, and re-layouts  40.1 us (22%)
  matrix products  21.3 us (12%)
  blocking collectives  21.1 us (12%)
  other arithmetic  18 us (10%)
  between operations  14.1 us (8%)
  starting transfers between devices  7.74 us (4%)
    all_gather x1, waiting for transfers between devices, body(): part_rows = lax.all_gather(kv_local, 'blk', axis=1, tiled=True)  47 us
    gather x4, local copies, waits for them, and re-layouts, attend(): key_visit = jnp.take(visit_ids, key_pos)  17.9 us
    all_to_all x1, blocking collectives, body(): lax.all_to_all(attended_local, 'head', split_axis=0, concat_axis=1, tiled...  13.9 us
    dot_general x4, matrix products, attend(): jnp.einsum('qhgk,khd->qhgd', weights.astype(jnp.bfloat16), value_heads, p...  13.5 us
    reduce_sum x4, other arithmetic, attend(): new_total = run_total * factor + jnp.sum(weights, axis=-1)  12.4 us
    dot_general x4, matrix products, attend(): jnp.einsum('qhgd,khd->qhgk', grouped, key_heads, preferred_element_type=j...  7.83 us
    all_to_all x1, blocking collectives, body(): lax.all_to_all(value_rows, 'head', split_axis=1, concat_axis=0, tiled=True)  7.19 us
    while x28, local copies, waits for them, and re-layouts  6.74 us
  transfers between devices with their start and end apart: 3, of which 3 were waited for; matrix products, arithmetic and copies ran while one was open for 4% of the time, Pallas kernels for 0%

commit v1 on v0

--- a/solution.py
+++ b/solution.py
@@ -1,12 +1,20 @@
+import functools
+
 import jax
 import jax.numpy as jnp
 from jax import lax
+from jax.experimental import pallas as pl
+from jax.experimental.pallas import tpu as pltpu
 from jax.sharding import PartitionSpec as P
 
 HEADS = 32
 KV_HEADS = 8
 HEAD_DIM = 128
-
+VISITS = 4
+GROUP = HEADS // KV_HEADS
+LOG2E = 1.4426950408889634
+
+MESH = pl.DeviceIdType.MESH
 
 masked_score = -1e30
 
@@ -17,7 +25,7 @@
     return jnp.sum(picked, axis=1)
 
 
-def body(queries, key_rows, value_rows, visit_ids, span_order):
+def gathered_body(queries, key_rows, value_rows, visit_ids, span_order):
     head_queries, head_keys, head_values = (
         lax.all_to_all(queries, "head", split_axis=1, concat_axis=0, tiled=True),
         lax.all_to_all(key_rows, "head", split_axis=1, concat_axis=0, tiled=True),
@@ -88,6 +96,283 @@
     return lax.all_to_all(attended_local, "head", split_axis=0, concat_axis=1, tiled=True)
 
 
+def fused_kernel(
+    dims, q_ref, k_ref, v_ref, visit_ref, span_ref, out_ref,
+    kv, qs, outs, bias,
+    kv_recv, y_send, core_send, z_send, x_send, x_recv, own_sem, out_send, out_recv, out_own,
+):
+    nz, nh, rows, phases = dims
+    nblk = 4 * nz
+    block = nh * rows
+    keys = nblk * block
+    me = lax.axis_index("blk")
+    x = lax.axis_index("head")
+    z, y, core = me // 4, (me // 2) % 2, me % 2
+
+    def index_of(z_at, y_at, core_at):
+        return z_at * 4 + y_at * 2 + core_at
+
+    z_peers = [lax.rem(z + step, nz) for step in range(1, nz)]
+    z_ids = [index_of(zp, y, core) for zp in z_peers]
+    y_id = index_of(z, 1 - y, core)
+    core_id = index_of(z, y, 1 - core)
+    x_peers = [lax.rem(x + step, nh) for step in range(1, nh)]
+
+    barrier = pltpu.get_barrier_semaphore()
+    for blk in z_ids + [y_id, core_id]:
+        pl.semaphore_signal(barrier, inc=1, device_id=(blk, x), device_id_type=MESH)
+    for xp in x_peers:
+        pl.semaphore_signal(barrier, inc=1, device_id=(me, xp), device_id_type=MESH)
+
+    def sources(p, to):
+        kv_at = pl.multiple_of((to * phases + p) * HEAD_DIM, HEAD_DIM)
+        q_at = pl.multiple_of((to * phases + p) * GROUP * HEAD_DIM, GROUP * HEAD_DIM)
+        return (
+            k_ref.at[:, pl.ds(kv_at, HEAD_DIM)],
+            v_ref.at[:, pl.ds(kv_at, HEAD_DIM)],
+            q_ref.at[:, pl.ds(q_at, GROUP * HEAD_DIM)],
+        )
+
+    def landing(p, source):
+        row = pl.multiple_of(me * block + source * rows, 16)
+        return (
+            kv.at[p, 0, pl.ds(row, rows), :],
+            kv.at[p, 1, pl.ds(row, rows), :],
+            qs.at[p, source],
+        )
+
+    def own_copies(p):
+        return [
+            pltpu.make_async_copy(src, dst, own_sem.at[p, kind])
+            for kind, (src, dst) in enumerate(zip(sources(p, x), landing(p, x)))
+        ]
+
+    def x_copies(p, kinds):
+        result = []
+        for step, xp in enumerate(x_peers):
+            from_refs, to_refs = sources(p, xp), landing(p, x)
+            for kind in kinds:
+                result.append(
+                    pltpu.make_async_remote_copy(
+                        src_ref=from_refs[kind], dst_ref=to_refs[kind],
+                        send_sem=x_send.at[p, step, kind], recv_sem=x_recv.at[p, step, kind],
+                        device_id=(me, xp), device_id_type=MESH,
+                    )
+                )
+        return result
+
+    def block_ref(p, blk):
+        return kv.at[p, :, pl.ds(pl.multiple_of(blk * block, 16), block), :]
+
+    def gather_copy(p, blk, send_sem, target):
+        return pltpu.make_async_remote_copy(
+            src_ref=block_ref(p, blk), dst_ref=block_ref(p, blk),
+            send_sem=send_sem, recv_sem=kv_recv.at[p, blk],
+            device_id=(target, x), device_id_type=MESH,
+        )
+
+    sent = []
+
+    def send(copy):
+        copy.start()
+        sent.append(copy)
+
+    def await_block(p, blk):
+        gather_copy(p, blk, y_send.at[p, 0], y_id).wait_recv()
+
+    def start_own(p):
+        for copy in own_copies(p)[:2]:
+            copy.wait()
+        for copy in x_copies(p, (0, 1)):
+            copy.wait()
+        send(gather_copy(p, me, y_send.at[p, 0], y_id))
+        for step, blk in enumerate(z_ids):
+            send(gather_copy(p, me, z_send.at[p, step], blk))
+        send(gather_copy(p, me, core_send.at[p, 0], core_id))
+
+    def forward_z(p, step):
+        blk = index_of(lax.rem(z + nz - 1 - step, nz), y, core)
+        await_block(p, blk)
+        send(gather_copy(p, blk, y_send.at[p, 1 + step], y_id))
+        send(gather_copy(p, blk, core_send.at[p, 1 + step], core_id))
+
+    def forward_y(p):
+        for step in range(nz):
+            blk = index_of(lax.rem(z + nz - step, nz), 1 - y, core)
+            await_block(p, blk)
+            send(gather_copy(p, blk, core_send.at[p, nz + step], core_id))
+
+    def await_core(p):
+        for side in (y, 1 - y):
+            for step in range(nz):
+                await_block(p, index_of(lax.rem(z + nz - step, nz), side, 1 - core))
+
+    for p in range(phases):
+        for copy in own_copies(p):
+            copy.start()
+
+    query_pos = span_ref[me] * block + lax.broadcasted_iota(jnp.int32, (block, 1), 0)
+    first = jnp.zeros((block, 1), jnp.int32)
+    visits = visit_ref[...]
+    for visit in range(1, VISITS):
+        begin = jnp.sum(jnp.where(visits < visit, 1.0, 0.0), axis=1, keepdims=True)
+        begin = jnp.sum(begin, axis=0, keepdims=True).astype(jnp.int32)
+        first = jnp.where(begin <= query_pos, jnp.maximum(first, begin), first)
+    lane = lax.broadcasted_iota(jnp.int32, (1, 2 * block), 1)
+    for pair in range(nblk // 2):
+        key_pos = jnp.where(
+            lane < block,
+            span_ref[2 * pair] * block + lane,
+            span_ref[2 * pair + 1] * block + (lane - block),
+        )
+        allowed = (key_pos <= query_pos) & (key_pos >= first)
+        bias[:, 2 * block * pair : 2 * block * (pair + 1)] = jnp.where(allowed, 0.0, -jnp.inf)
+
+    pl.semaphore_wait(barrier, nz + 1 + nh - 1)
+
+    for copy in x_copies(0, (0, 1, 2)):
+        copy.start()
+    for p in range(1, min(2, phases)):
+        for copy in x_copies(p, (0, 1, 2)):
+            copy.start()
+    start_own(0)
+
+    chunk = next(size for size in (512, 384, 256, 128) if keys % size == 0)
+    batch = 2
+    scale = HEAD_DIM**-0.5 * LOG2E
+    lowest = -3.0e38
+
+    def compute(p, part):
+        at = part * batch
+        query = jnp.concatenate(
+            [
+                jnp.concatenate([qs[p, h, :, g * HEAD_DIM : (g + 1) * HEAD_DIM] for h in range(nh)], axis=0)
+                for g in range(at, at + batch)
+            ],
+            axis=0,
+        )
+
+        def step(index, state):
+            run_max, run_acc = state
+            start = pl.multiple_of(index * chunk, chunk)
+            key = kv[p, 0, pl.ds(start, chunk), :]
+            value = kv[p, 1, pl.ds(start, chunk), :]
+            extended = jnp.concatenate([value, jnp.ones_like(value)], axis=1)
+            score = lax.dot_general(
+                query, key, (((1,), (1,)), ((), ())), preferred_element_type=jnp.float32
+            )
+            mask = bias[:, pl.ds(start, chunk)]
+            shifted = jnp.concatenate(
+                [score[i * block : (i + 1) * block] * scale + mask for i in range(batch)], axis=0
+            )
+            new_max = jnp.maximum(run_max, jnp.max(shifted, axis=1, keepdims=True))
+            weight = jnp.exp2(shifted - new_max).astype(jnp.bfloat16)
+            factor = jnp.exp2(run_max - new_max)
+            new_acc = run_acc * factor + jnp.dot(
+                weight, extended, preferred_element_type=jnp.float32
+            )
+            return new_max, new_acc
+
+        initial = (
+            jnp.full((batch * block, 1), lowest, jnp.float32),
+            jnp.zeros((batch * block, 2 * HEAD_DIM), jnp.float32),
+        )
+        _, acc = lax.fori_loop(0, keys // chunk, step, initial)
+        result = (acc[:, :HEAD_DIM] / acc[:, HEAD_DIM:]).astype(jnp.bfloat16)
+        for i in range(batch):
+            for h in range(nh):
+                first_row = i * block + h * rows
+                outs[p, h, :, (at + i) * HEAD_DIM : (at + i + 1) * HEAD_DIM] = result[
+                    first_row : first_row + rows
+                ]
+
+    width = GROUP * HEAD_DIM
+
+    def out_copies(p):
+        place = out_ref.at[:, pl.ds(pl.multiple_of((x * phases + p) * width, width), width)]
+        copies = [pltpu.make_async_copy(outs.at[p, x], place, out_own.at[p])]
+        for step, xp in enumerate(x_peers):
+            copies.append(
+                pltpu.make_async_remote_copy(
+                    src_ref=outs.at[p, xp], dst_ref=place,
+                    send_sem=out_send.at[p, step], recv_sem=out_recv.at[p, step],
+                    device_id=(me, xp), device_id_type=MESH,
+                )
+            )
+        return copies
+
+    for step in range(nz - 1):
+        forward_z(0, step)
+    for p in range(phases):
+        more = p + 1 < phases
+        if more:
+            start_own(p + 1)
+        if p + 2 < phases:
+            for copy in x_copies(p + 2, (0, 1, 2)):
+                copy.start()
+        forward_y(p)
+        own_copies(p)[2].wait()
+        for copy in x_copies(p, (2,)):
+            copy.wait()
+        await_core(p)
+        parts = GROUP // batch
+        passed = 0
+        for part in range(parts):
+            compute(p, part)
+            upto = (nz - 1) * (part + 1) // parts
+            while more and passed < upto:
+                forward_z(p + 1, passed)
+                passed += 1
+        for copy in out_copies(p):
+            copy.start()
+    for p in range(phases):
+        for copy in out_copies(p):
+            copy.wait()
+    for copy in sent:
+        copy.wait_send()
+
+
+def fused_body(nblk, nh, queries, key_rows, value_rows, visit_ids, span_order):
+    rows = queries.shape[0]
+    block = rows * nh
+    phases = KV_HEADS // nh
+    nz = nblk // 4
+    dma = pltpu.SemaphoreType.DMA
+    any_spec = pl.BlockSpec(memory_space=pl.ANY)
+    return pl.pallas_call(
+        functools.partial(fused_kernel, (nz, nh, rows, phases)),
+        out_shape=jax.ShapeDtypeStruct(queries.shape, jnp.bfloat16),
+        in_specs=[
+            any_spec,
+            any_spec,
+            any_spec,
+            pl.BlockSpec(memory_space=pltpu.VMEM),
+            pl.BlockSpec(memory_space=pltpu.SMEM),
+        ],
+        out_specs=pl.BlockSpec(memory_space=pltpu.VMEM),
+        scratch_shapes=[
+            pltpu.VMEM((phases, 2, nblk * block, HEAD_DIM), jnp.bfloat16),
+            pltpu.VMEM((phases, nh, rows, GROUP * HEAD_DIM), jnp.bfloat16),
+            pltpu.VMEM((phases, nh, rows, GROUP * HEAD_DIM), jnp.bfloat16),
+            pltpu.VMEM((block, nblk * block), jnp.float32),
+            dma((phases, nblk)),
+            dma((phases, nz)),
+            dma((phases, 2 * nz)),
+            dma((phases, nz - 1)),
+            dma((phases, nh - 1, 3)),
+            dma((phases, nh - 1, 3)),
+            dma((phases, 3)),
+            dma((phases, nh - 1)),
+            dma((phases, nh - 1)),
+            dma((phases,)),
+        ],
+        compiler_params=pltpu.CompilerParams(
+            collective_id=0, has_side_effects=True, vmem_limit_bytes=48 * 2**20
+        ),
+        name="visit_attention",
+    )(queries, key_rows, value_rows, visit_ids.reshape(-1, 128), span_order)
+
+
 def solution(mesh):
     placed = (
         P(("blk", "head"), None),
@@ -96,6 +381,13 @@
         P(),
         P(),
     )
+    nblk, nh = mesh.shape["blk"], mesh.shape["head"]
+
+    def body(queries, *rest):
+        if queries.shape[0] % 16 == 0 and nblk % 4 == 0 and KV_HEADS % nh == 0:
+            return fused_body(nblk, nh, queries, *rest)
+        return gathered_body(queries, *rest)
+
     return jax.shard_map(
         body, mesh=mesh, in_specs=placed, out_specs=P(("blk", "head"), None), check_vma=False
     )

time: 180 us -> 90.2 us (0.50)
  Pallas kernels: 0 us -> 84 us
  waiting for transfers between devices: 56.6 us -> 0 us
  local copies, waits for them, and re-layouts: 40.1 us -> 5.23 us
  matrix products: 21.3 us -> 0 us
  blocking collectives: 21.1 us -> 0 us
  other arithmetic: 18 us -> 0 us
  between operations: 14.1 us -> 0.01 us
  starting transfers between devices: 7.74 us -> 0 us
    pallas_call x0 -> x1, Pallas kernels: none -> 84 us  [fused_body(): pl.pallas_call(functools.partial(fused_kernel, (nz, nh, rows, phases)), o...]
    all_gather x1 -> x0, waiting for transfers between devices: 47 us -> none  [body(): part_rows = lax.all_gather(kv_local, 'blk', axis=1, tiled=True)]
    dot_general x8 -> x0, matrix products: 21.3 us -> none  [the longest x4 13.5 us: attend(): jnp.einsum('qhgk,khd->qhgd', weights.astype(jnp.bfloat16), value_heads, p...]
    all_to_all x2 -> x0, blocking collectives: 21.1 us -> none  [the longest x1 13.9 us: body(): lax.all_to_all(attended_local, 'head', split_axis=0, concat_axis=1, tiled...]
    gather x5 -> x0, local copies, waits for them, and re-layouts: 19.8 us -> none  [the longest x4 17.9 us: attend(): key_visit = jnp.take(visit_ids, key_pos)]
    reduce_sum x9 -> x0, other arithmetic: 14.1 us -> none  [the longest x4 12.4 us: attend(): new_total = run_total * factor + jnp.sum(weights, axis=-1)]
    all_to_all x2 -> x0, waiting for transfers between devices: 9.57 us -> none  [the longest x1 5.36 us: body(): lax.all_to_all(queries, 'head', split_axis=1, concat_axis=0, tiled=True)]
    all_to_all x2 -> x0, starting transfers between devices: 7.74 us -> none  [the longest x1 4.21 us: body(): lax.all_to_all(key_rows, 'head', split_axis=1, concat_axis=0, tiled=True)]
  transfers between devices with their start and end apart: 3 -> 0, of which waited for: 3 -> 0; matrix products, arithmetic and copies ran while one was open for 4% -> 0% of each run, Pallas kernels for 0% -> 0%
where the time goes in v1:
time: 90.2 us; the launch traced here: 89.3 us
  Pallas kernels  84 us (93%)
  local copies, waits for them, and re-layouts  5.23 us (6%)
    pallas_call x1, Pallas kernels, fused_body(): pl.pallas_call(functools.partial(fused_kernel, (nz, nh, rows, phases)), o...  84 us
    unnamed x11, local copies, waits for them, and re-layouts  5.23 us

profile of v1, /device:TPU:0, one launch (start us, length us, event | category | flops | bytes accessed | tf_op | source)
XLA Modules:
  0.0 89.3 jit_solution(8695720682900950222)
XLA Ops:
  0.0 0.0 copy-start.4
  0.0 0.7 copy-done.4
  0.7 0.0 copy-start
  0.7 1.1 %copy-done = bf16[96,4096]{1,0:T(8,128)(2,1)S(1)} copy-done((bf16[96,4096]{1,0:T(8,128)(2,1)S(1)}, bf16[96,4096]{1,0:T(8,128)(2,1)}, u32[]{:S(2)}) %copy-start) | copy-done | bytes 786456
  1.8 0.0 copy-start.1
  1.8 0.9 %copy-done.1 = bf16[96,1024]{1,0:T(8,128)(2,1)S(1)} copy-done((bf16[96,1024]{1,0:T(8,128)(2,1)S(1)}, bf16[96,1024]{1,0:T(8,128)(2,1)}, u32[]{:S(2)}) %copy-start.1) | copy-done | bytes 196632
  2.7 0.0 copy-start.2
  2.7 0.9 %copy-done.2 = bf16[96,1024]{1,0:T(8,128)(2,1)S(1)} copy-done((bf16[96,1024]{1,0:T(8,128)(2,1)S(1)}, bf16[96,1024]{1,0:T(8,128)(2,1)}, u32[]{:S(2)}) %copy-start.2) | copy-done | bytes 196632
  3.6 0.0 copy-start.3
  3.6 0.7 copy-done.3
  4.4 84.0 %visit_attention.1 = bf16[96,4096]{1,0:T(8,128)(2,1)S(1)} custom-call(bf16[96,4096]{1,0:T(8,128)(2,1)S(1)} %copy-done, bf16[96,1024]{1,0:T(8,128)(2,1)S(1)} %copy-done.1, bf16[96,1024]{1,0:T(8,128)(2,1)S(1)} %copy-done.2, s32[24,128]{1,0:T(8,128)S(1)} %bitcast.1, s32[16]{0:T(128)S(1)} %copy-done.4), custom_call_target="tpu_custom_call" | custom-call | tf_op jit(solution)/shard_map/visit_attention/pallas_call | solution.py:342
  88.4 0.9 copy.7
Async XLA Ops:
  0.0 0.7 copy-start.4
  0.7 1.1 %copy-start = (bf16[96,4096]{1,0:T(8,128)(2,1)S(1)}, bf16[96,4096]{1,0:T(8,128)(2,1)}, u32[]{:S(2)}) copy-start(bf16[96,4096]{1,0:T(8,128)(2,1)} %q_ref.1) | copy-start | bytes 2359300
  1.8 0.9 %copy-start.1 = (bf16[96,1024]{1,0:T(8,128)(2,1)S(1)}, bf16[96,1024]{1,0:T(8,128)(2,1)}, u32[]{:S(2)}) copy-start(bf16[96,1024]{1,0:T(8,128)(2,1)} %k_ref.1) | copy-start | bytes 589828
  2.7 0.9 %copy-start.2 = (bf16[96,1024]{1,0:T(8,128)(2,1)S(1)}, bf16[96,1024]{1,0:T(8,128)(2,1)}, u32[]{:S(2)}) copy-start(bf16[96,1024]{1,0:T(8,128)(2,1)} %v_ref.1) | copy-start | bytes 589828
  3.6 0.7 copy-start.3

commit v2 on v1

--- a/solution.py
+++ b/solution.py
@@ -141,10 +141,11 @@
             qs.at[p, source],
         )
 
-    def own_copies(p):
+    def own_copies(p, kinds=3, first_kind=0):
+        pairs = list(zip(sources(p, x), landing(p, x)))
         return [
-            pltpu.make_async_copy(src, dst, own_sem.at[p, kind])
-            for kind, (src, dst) in enumerate(zip(sources(p, x), landing(p, x)))
+            pltpu.make_async_copy(*pairs[kind], own_sem.at[p, kind])
+            for kind in range(first_kind, kinds)
         ]
 
     def x_copies(p, kinds):
@@ -171,36 +172,48 @@
             device_id=(target, x), device_id_type=MESH,
         )
 
-    sent = []
-
-    def send(copy):
-        copy.start()
-        sent.append(copy)
-
     def await_block(p, blk):
         gather_copy(p, blk, y_send.at[p, 0], y_id).wait_recv()
 
+    def own_sends(p):
+        copies = [gather_copy(p, me, y_send.at[p, 0], y_id)]
+        for step, blk in enumerate(z_ids):
+            copies.append(gather_copy(p, me, z_send.at[p, step], blk))
+        copies.append(gather_copy(p, me, core_send.at[p, 0], core_id))
+        return copies
+
     def start_own(p):
-        for copy in own_copies(p)[:2]:
+        for copy in own_copies(p, 2):
             copy.wait()
         for copy in x_copies(p, (0, 1)):
             copy.wait()
-        send(gather_copy(p, me, y_send.at[p, 0], y_id))
-        for step, blk in enumerate(z_ids):
-            send(gather_copy(p, me, z_send.at[p, step], blk))
-        send(gather_copy(p, me, core_send.at[p, 0], core_id))
+        for copy in own_sends(p):
+            copy.start()
+
+    def z_block(step):
+        return index_of(lax.rem(z + nz - 1 - step, nz), y, core)
+
+    def z_forwards(p, step):
+        blk = z_block(step)
+        return [
+            gather_copy(p, blk, y_send.at[p, 1 + step], y_id),
+            gather_copy(p, blk, core_send.at[p, 1 + step], core_id),
+        ]
 
     def forward_z(p, step):
-        blk = index_of(lax.rem(z + nz - 1 - step, nz), y, core)
-        await_block(p, blk)
-        send(gather_copy(p, blk, y_send.at[p, 1 + step], y_id))
-        send(gather_copy(p, blk, core_send.at[p, 1 + step], core_id))
-
-    def forward_y(p):
-        for step in range(nz):
-            blk = index_of(lax.rem(z + nz - step, nz), 1 - y, core)
-            await_block(p, blk)
-            send(gather_copy(p, blk, core_send.at[p, nz + step], core_id))
+        await_block(p, z_block(step))
+        for copy in z_forwards(p, step):
+            copy.start()
+
+    def y_block(step):
+        return index_of(lax.rem(z + nz - step, nz), 1 - y, core)
+
+    def y_forward(p, step):
+        return gather_copy(p, y_block(step), core_send.at[p, nz + step], core_id)
+
+    def forward_y(p, step):
+        await_block(p, y_block(step))
+        y_forward(p, step).start()
 
     def await_core(p):
         for side in (y, 1 - y):
@@ -230,19 +243,19 @@
 
     pl.semaphore_wait(barrier, nz + 1 + nh - 1)
 
-    for copy in x_copies(0, (0, 1, 2)):
-        copy.start()
-    for p in range(1, min(2, phases)):
-        for copy in x_copies(p, (0, 1, 2)):
+    for p in range(phases):
+        for copy in x_copies(p, (0, 1)):
             copy.start()
-    start_own(0)
+    for p in range(phases):
+        for copy in x_copies(p, (2,)):
+            copy.start()
 
     chunk = next(size for size in (512, 384, 256, 128) if keys % size == 0)
     batch = 2
     scale = HEAD_DIM**-0.5 * LOG2E
     lowest = -3.0e38
 
-    def compute(p, part):
+    def compute(p, part, events):
         at = part * batch
         query = jnp.concatenate(
             [
@@ -253,6 +266,8 @@
         )
 
         def step(index, state):
+            for slot, event in events:
+                pl.when(index == slot)(event)
             run_max, run_acc = state
             start = pl.multiple_of(index * chunk, chunk)
             key = kv[p, 0, pl.ds(start, chunk), :]
@@ -286,50 +301,64 @@
                     first_row : first_row + rows
                 ]
 
-    width = GROUP * HEAD_DIM
-
-    def out_copies(p):
-        place = out_ref.at[:, pl.ds(pl.multiple_of((x * phases + p) * width, width), width)]
-        copies = [pltpu.make_async_copy(outs.at[p, x], place, out_own.at[p])]
+    width = batch * HEAD_DIM
+    parts = GROUP // batch
+
+    def out_copies(p, part):
+        at = pl.multiple_of(((x * phases + p) * parts + part) * width, width)
+        place = out_ref.at[:, pl.ds(at, width)]
+        held = pl.ds(part * width, width)
+        copies = [pltpu.make_async_copy(outs.at[p, x, :, held], place, out_own.at[p, part])]
         for step, xp in enumerate(x_peers):
             copies.append(
                 pltpu.make_async_remote_copy(
-                    src_ref=outs.at[p, xp], dst_ref=place,
-                    send_sem=out_send.at[p, step], recv_sem=out_recv.at[p, step],
+                    src_ref=outs.at[p, xp, :, held], dst_ref=place,
+                    send_sem=out_send.at[p, part, step], recv_sem=out_recv.at[p, part, step],
                     device_id=(me, xp), device_id_type=MESH,
                 )
             )
         return copies
 
+    chunks = keys // chunk
+    slots = chunks * parts
+
+    def events_of(p):
+        events = [functools.partial(forward_y, p, 0)]
+        events += [functools.partial(forward_z, p, step) for step in range(nz - 1)]
+        return [(min(slots - 1, (k + 1) * slots // (len(events) + 1)), e) for k, e in enumerate(events)]
+
+    for p in range(min(2, phases)):
+        start_own(p)
     for step in range(nz - 1):
         forward_z(0, step)
+    forward_y(0, 0)
     for p in range(phases):
-        more = p + 1 < phases
-        if more:
-            start_own(p + 1)
         if p + 2 < phases:
-            for copy in x_copies(p + 2, (0, 1, 2)):
-                copy.start()
-        forward_y(p)
-        own_copies(p)[2].wait()
+            start_own(p + 2)
+        for step in range(1, nz):
+            forward_y(p, step)
+        for copy in own_copies(p, 3, 2):
+            copy.wait()
         for copy in x_copies(p, (2,)):
             copy.wait()
         await_core(p)
-        parts = GROUP // batch
-        passed = 0
+        events = events_of(p + 1) if p + 1 < phases else []
         for part in range(parts):
-            compute(p, part)
-            upto = (nz - 1) * (part + 1) // parts
-            while more and passed < upto:
-                forward_z(p + 1, passed)
-                passed += 1
-        for copy in out_copies(p):
-            copy.start()
+            low = part * chunks
+            compute(p, part, [(slot - low, e) for slot, e in events if low <= slot < low + chunks])
+            for copy in out_copies(p, part):
+                copy.start()
     for p in range(phases):
-        for copy in out_copies(p):
-            copy.wait()
-    for copy in sent:
-        copy.wait_send()
+        for part in range(parts):
+            for copy in out_copies(p, part):
+                copy.wait()
+        for copy in own_sends(p):
+            copy.wait_send()
+        for step in range(nz - 1):
+            for copy in z_forwards(p, step):
+                copy.wait_send()
+        for step in range(nz):
+            y_forward(p, step).wait_send()
 
 
 def fused_body(nblk, nh, queries, key_rows, value_rows, visit_ids, span_order):
@@ -362,12 +391,12 @@
             dma((phases, nh - 1, 3)),
             dma((phases, nh - 1, 3)),
             dma((phases, 3)),
-            dma((phases, nh - 1)),
-            dma((phases, nh - 1)),
-            dma((phases,)),
+            dma((phases, GROUP, nh - 1)),
+            dma((phases, GROUP, nh - 1)),
+            dma((phases, GROUP)),
         ],
         compiler_params=pltpu.CompilerParams(
-            collective_id=0, has_side_effects=True, vmem_limit_bytes=48 * 2**20
+            collective_id=0, has_side_effects=True, vmem_limit_bytes=60 * 2**20
         ),
         name="visit_attention",
     )(queries, key_rows, value_rows, visit_ids.reshape(-1, 128), span_order)

time: 90.2 us -> 81.5 us (0.904)
  Pallas kernels: 84 us -> 77.9 us
  local copies, waits for them, and re-layouts: 5.23 us -> 2.06 us
    pallas_call x1, Pallas kernels: 84 us -> 77.9 us  [fused_body(): pl.pallas_call(functools.partial(fused_kernel, (nz, nh, rows, phases)), o...]
    unnamed x11 -> x1, local copies, waits for them, and re-layouts: 5.23 us -> 2.06 us
where the time goes in v2:
time: 81.5 us; the launch traced here: 80 us
  Pallas kernels  77.9 us (96%)
  local copies, waits for them, and re-layouts  2.06 us (3%)
    pallas_call x1, Pallas kernels, fused_body(): pl.pallas_call(functools.partial(fused_kernel, (nz, nh, rows, phases)), o...  77.9 us
    unnamed x1, local copies, waits for them, and re-layouts  2.06 us

profile of v2, /device:TPU:0, one launch (start us, length us, event | category | flops | bytes accessed | tf_op | source)
XLA Modules:
  0.0 80.0 jit_solution(5974894837341208237)
XLA Ops:
  0.0 77.9 %visit_attention.1 = bf16[96,4096]{1,0:T(8,128)(2,1)} custom-call(bf16[96,4096]{1,0:T(8,128)(2,1)} %q_ref.1, bf16[96,1024]{1,0:T(8,128)(2,1)} %k_ref.1, bf16[96,1024]{1,0:T(8,128)(2,1)} %v_ref.1, s32[24,128]{1,0:T(8,128)} %bitcast.1, s32[16]{0:T(128)} %span_ref.1), custom_call_target="tpu_custom_call" | custom-call | tf_op jit(solution)/shard_map/visit_attention/pallas_call | solution.py:371
  78.0 2.1 %copy.7 = bf16[96,4096]{1,0:T(8,128)(2,1)} copy(bf16[96,4096]{1,0:T(8,128)(2,1)} %visit_attention.1) | data formatting | bytes 1572864

commit v3 on v2

--- a/solution.py
+++ b/solution.py
@@ -12,7 +12,6 @@
 HEAD_DIM = 128
 VISITS = 4
 GROUP = HEADS // KV_HEADS
-LOG2E = 1.4426950408889634
 
 MESH = pl.DeviceIdType.MESH
 
@@ -96,10 +95,9 @@
     return lax.all_to_all(attended_local, "head", split_axis=0, concat_axis=1, tiled=True)
 
 
-def fused_kernel(
-    dims, q_ref, k_ref, v_ref, visit_ref, span_ref, out_ref,
-    kv, qs, outs, bias,
-    kv_recv, y_send, core_send, z_send, x_send, x_recv, own_sem, out_send, out_recv, out_own,
+def gather_kernel(
+    dims, q_ref, k_ref, v_ref, kv, qs,
+    kv_recv, y_send, core_send, z_send, x_send, x_recv, own_sem,
 ):
     nz, nh, rows, phases = dims
     nblk = 4 * nz
@@ -224,23 +222,6 @@
         for copy in own_copies(p):
             copy.start()
 
-    query_pos = span_ref[me] * block + lax.broadcasted_iota(jnp.int32, (block, 1), 0)
-    first = jnp.zeros((block, 1), jnp.int32)
-    visits = visit_ref[...]
-    for visit in range(1, VISITS):
-        begin = jnp.sum(jnp.where(visits < visit, 1.0, 0.0), axis=1, keepdims=True)
-        begin = jnp.sum(begin, axis=0, keepdims=True).astype(jnp.int32)
-        first = jnp.where(begin <= query_pos, jnp.maximum(first, begin), first)
-    lane = lax.broadcasted_iota(jnp.int32, (1, 2 * block), 1)
-    for pair in range(nblk // 2):
-        key_pos = jnp.where(
-            lane < block,
-            span_ref[2 * pair] * block + lane,
-            span_ref[2 * pair + 1] * block + (lane - block),
-        )
-        allowed = (key_pos <= query_pos) & (key_pos >= first)
-        bias[:, 2 * block * pair : 2 * block * (pair + 1)] = jnp.where(allowed, 0.0, -jnp.inf)
-
     pl.semaphore_wait(barrier, nz + 1 + nh - 1)
 
     for p in range(phases):
@@ -250,108 +231,22 @@
         for copy in x_copies(p, (2,)):
             copy.start()
 
-    chunk = next(size for size in (512, 384, 256, 128) if keys % size == 0)
-    batch = 2
-    scale = HEAD_DIM**-0.5 * LOG2E
-    lowest = -3.0e38
-
-    def compute(p, part, events):
-        at = part * batch
-        query = jnp.concatenate(
-            [
-                jnp.concatenate([qs[p, h, :, g * HEAD_DIM : (g + 1) * HEAD_DIM] for h in range(nh)], axis=0)
-                for g in range(at, at + batch)
-            ],
-            axis=0,
-        )
-
-        def step(index, state):
-            for slot, event in events:
-                pl.when(index == slot)(event)
-            run_max, run_acc = state
-            start = pl.multiple_of(index * chunk, chunk)
-            key = kv[p, 0, pl.ds(start, chunk), :]
-            value = kv[p, 1, pl.ds(start, chunk), :]
-            extended = jnp.concatenate([value, jnp.ones_like(value)], axis=1)
-            score = lax.dot_general(
-                query, key, (((1,), (1,)), ((), ())), preferred_element_type=jnp.float32
-            )
-            mask = bias[:, pl.ds(start, chunk)]
-            shifted = jnp.concatenate(
-                [score[i * block : (i + 1) * block] * scale + mask for i in range(batch)], axis=0
-            )
-            new_max = jnp.maximum(run_max, jnp.max(shifted, axis=1, keepdims=True))
-            weight = jnp.exp2(shifted - new_max).astype(jnp.bfloat16)
-            factor = jnp.exp2(run_max - new_max)
-            new_acc = run_acc * factor + jnp.dot(
-                weight, extended, preferred_element_type=jnp.float32
-            )
-            return new_max, new_acc
-
-        initial = (
-            jnp.full((batch * block, 1), lowest, jnp.float32),
-            jnp.zeros((batch * block, 2 * HEAD_DIM), jnp.float32),
-        )
-        _, acc = lax.fori_loop(0, keys // chunk, step, initial)
-        result = (acc[:, :HEAD_DIM] / acc[:, HEAD_DIM:]).astype(jnp.bfloat16)
-        for i in range(batch):
-            for h in range(nh):
-                first_row = i * block + h * rows
-                outs[p, h, :, (at + i) * HEAD_DIM : (at + i + 1) * HEAD_DIM] = result[
-                    first_row : first_row + rows
-                ]
-
-    width = batch * HEAD_DIM
-    parts = GROUP // batch
-
-    def out_copies(p, part):
-        at = pl.multiple_of(((x * phases + p) * parts + part) * width, width)
-        place = out_ref.at[:, pl.ds(at, width)]
-        held = pl.ds(part * width, width)
-        copies = [pltpu.make_async_copy(outs.at[p, x, :, held], place, out_own.at[p, part])]
-        for step, xp in enumerate(x_peers):
-            copies.append(
-                pltpu.make_async_remote_copy(
-                    src_ref=outs.at[p, xp, :, held], dst_ref=place,
-                    send_sem=out_send.at[p, part, step], recv_sem=out_recv.at[p, part, step],
-                    device_id=(me, xp), device_id_type=MESH,
-                )
-            )
-        return copies
-
-    chunks = keys // chunk
-    slots = chunks * parts
-
-    def events_of(p):
-        events = [functools.partial(forward_y, p, 0)]
-        events += [functools.partial(forward_z, p, step) for step in range(nz - 1)]
-        return [(min(slots - 1, (k + 1) * slots // (len(events) + 1)), e) for k, e in enumerate(events)]
-
     for p in range(min(2, phases)):
         start_own(p)
-    for step in range(nz - 1):
-        forward_z(0, step)
-    forward_y(0, 0)
     for p in range(phases):
         if p + 2 < phases:
             start_own(p + 2)
+        forward_y(p, 0)
+        for step in range(nz - 1):
+            forward_z(p, step)
         for step in range(1, nz):
             forward_y(p, step)
+    for p in range(phases):
+        await_core(p)
         for copy in own_copies(p, 3, 2):
             copy.wait()
         for copy in x_copies(p, (2,)):
             copy.wait()
-        await_core(p)
-        events = events_of(p + 1) if p + 1 < phases else []
-        for part in range(parts):
-            low = part * chunks
-            compute(p, part, [(slot - low, e) for slot, e in events if low <= slot < low + chunks])
-            for copy in out_copies(p, part):
-                copy.start()
-    for p in range(phases):
-        for part in range(parts):
-            for copy in out_copies(p, part):
-                copy.wait()
         for copy in own_sends(p):
             copy.wait_send()
         for step in range(nz - 1):
@@ -361,6 +256,99 @@
             y_forward(p, step).wait_send()
 
 
+def attend_kernel(dims, meta_ref, order_ref, visit_ref, qs, kv, outs):
+    nz, nh, rows, phases = dims
+    block = nh * rows
+    scale = HEAD_DIM**-0.5
+    lowest = -3.0e38
+    my_span, low_span = meta_ref[0], meta_ref[1]
+
+    query_pos = my_span * block + lax.broadcasted_iota(jnp.int32, (block, 1), 0)
+    first = jnp.zeros((block, 1), jnp.int32)
+    visits = visit_ref[...]
+    for visit in range(1, VISITS):
+        begin = jnp.sum(jnp.where(visits < visit, 1.0, 0.0), axis=1, keepdims=True)
+        begin = jnp.sum(begin, axis=0, keepdims=True).astype(jnp.int32)
+        first = jnp.where(begin <= query_pos, jnp.maximum(first, begin), first)
+    lane = lax.broadcasted_iota(jnp.int32, (1, block), 1)
+
+    def one_head(p, carry):
+        query = jnp.concatenate(
+            [
+                jnp.concatenate([qs[p, h, :, g * HEAD_DIM : (g + 1) * HEAD_DIM] for h in range(nh)], axis=0)
+                for g in range(GROUP)
+            ],
+            axis=0,
+        )
+
+        def step(span, state):
+            run_max, run_acc = state
+            start = pl.multiple_of(order_ref[span] * block, 64)
+            key = kv[p, 0, pl.ds(start, block), :]
+            value = kv[p, 1, pl.ds(start, block), :]
+            extended = jnp.concatenate([value, jnp.ones_like(value)], axis=1)
+            score = lax.dot_general(
+                query, key, (((1,), (1,)), ((), ())), preferred_element_type=jnp.float32
+            )
+            key_pos = span * block + lane
+            mask = jnp.where((key_pos <= query_pos) & (key_pos >= first), 0.0, -jnp.inf)
+            shifted = jnp.concatenate(
+                [score[i * block : (i + 1) * block] * scale + mask for i in range(GROUP)], axis=0
+            )
+            new_max = jnp.maximum(run_max, jnp.max(shifted, axis=1, keepdims=True))
+            weight = jnp.exp(shifted - new_max).astype(jnp.bfloat16)
+            factor = jnp.exp(run_max - new_max)
+            new_acc = run_acc * factor + jnp.dot(
+                weight, extended, preferred_element_type=jnp.float32
+            )
+            return new_max, new_acc
+
+        initial = (
+            jnp.full((GROUP * block, 1), lowest, jnp.float32),
+            jnp.zeros((GROUP * block, 2 * HEAD_DIM), jnp.float32),
+        )
+        _, acc = lax.fori_loop(low_span, my_span + 1, step, initial)
+        result = (acc[:, :HEAD_DIM] / acc[:, HEAD_DIM:]).astype(jnp.bfloat16)
+        for i in range(GROUP):
+            for h in range(nh):
+                first_row = i * block + h * rows
+                outs[p, h, :, i * HEAD_DIM : (i + 1) * HEAD_DIM] = result[
+                    first_row : first_row + rows
+                ]
+        return carry
+
+    lax.fori_loop(0, phases, one_head, 0)
+
+
+def exchange_kernel(dims, outs, out_ref, out_own, out_send, out_recv):
+    nz, nh, rows, phases = dims
+    me = lax.axis_index("blk")
+    x = lax.axis_index("head")
+    x_peers = [lax.rem(x + step, nh) for step in range(1, nh)]
+    barrier = pltpu.get_barrier_semaphore()
+    for xp in x_peers:
+        pl.semaphore_signal(barrier, inc=1, device_id=(me, xp), device_id_type=MESH)
+    pl.semaphore_wait(barrier, nh - 1)
+    width = GROUP * HEAD_DIM
+    copies = []
+    for p in range(phases):
+        at = pl.multiple_of((x * phases + p) * width, width)
+        place = out_ref.at[:, pl.ds(at, width)]
+        copies.append(pltpu.make_async_copy(outs.at[p, x], place, out_own.at[p]))
+        for step, xp in enumerate(x_peers):
+            copies.append(
+                pltpu.make_async_remote_copy(
+                    src_ref=outs.at[p, xp], dst_ref=place,
+                    send_sem=out_send.at[p, step], recv_sem=out_recv.at[p, step],
+                    device_id=(me, xp), device_id_type=MESH,
+                )
+            )
+    for copy in copies:
+        copy.start()
+    for copy in copies:
+        copy.wait()
+
+
 def fused_body(nblk, nh, queries, key_rows, value_rows, visit_ids, span_order):
     rows = queries.shape[0]
     block = rows * nh
@@ -368,22 +356,17 @@
     nz = nblk // 4
     dma = pltpu.SemaphoreType.DMA
     any_spec = pl.BlockSpec(memory_space=pl.ANY)
-    return pl.pallas_call(
-        functools.partial(fused_kernel, (nz, nh, rows, phases)),
-        out_shape=jax.ShapeDtypeStruct(queries.shape, jnp.bfloat16),
-        in_specs=[
-            any_spec,
-            any_spec,
-            any_spec,
-            pl.BlockSpec(memory_space=pltpu.VMEM),
-            pl.BlockSpec(memory_space=pltpu.SMEM),
-        ],
-        out_specs=pl.BlockSpec(memory_space=pltpu.VMEM),
+    dims = (nz, nh, rows, phases)
+    keys = nblk * block
+    kv, qs = pl.pallas_call(
+        functools.partial(gather_kernel, dims),
+        out_shape=(
+            jax.ShapeDtypeStruct((phases, 2, keys, HEAD_DIM), jnp.bfloat16),
+            jax.ShapeDtypeStruct((phases, nh, rows, GROUP * HEAD_DIM), jnp.bfloat16),
+        ),
+        in_specs=[any_spec, any_spec, any_spec],
+        out_specs=(any_spec, any_spec),
         scratch_shapes=[
-            pltpu.VMEM((phases, 2, nblk * block, HEAD_DIM), jnp.bfloat16),
-            pltpu.VMEM((phases, nh, rows, GROUP * HEAD_DIM), jnp.bfloat16),
-            pltpu.VMEM((phases, nh, rows, GROUP * HEAD_DIM), jnp.bfloat16),
-            pltpu.VMEM((block, nblk * block), jnp.float32),
             dma((phases, nblk)),
             dma((phases, nz)),
             dma((phases, 2 * nz)),
@@ -391,15 +374,39 @@
             dma((phases, nh - 1, 3)),
             dma((phases, nh - 1, 3)),
             dma((phases, 3)),
-            dma((phases, GROUP, nh - 1)),
-            dma((phases, GROUP, nh - 1)),
-            dma((phases, GROUP)),
         ],
         compiler_params=pltpu.CompilerParams(
             collective_id=0, has_side_effects=True, vmem_limit_bytes=60 * 2**20
         ),
-        name="visit_attention",
-    )(queries, key_rows, value_rows, visit_ids.reshape(-1, 128), span_order)
+        name="gather_heads",
+    )(queries, key_rows, value_rows)
+    blocks = jnp.arange(nblk, dtype=jnp.int32)
+    order = jnp.sum(jnp.where(span_order[None, :] == blocks[:, None], blocks[None, :], 0), axis=1)
+    my_span = jnp.sum(jnp.where(blocks == lax.axis_index("blk"), span_order, 0))
+    begins = [jnp.sum((visit_ids < visit).astype(jnp.int32)) for visit in range(1, VISITS)]
+    low = jnp.int32(0)
+    for begin in begins:
+        low = jnp.where(begin <= my_span * block, jnp.maximum(low, begin), low)
+    meta = jnp.stack([my_span, low // block]).astype(jnp.int32)
+    smem = pl.BlockSpec(memory_space=pltpu.SMEM)
+    vmem = pl.BlockSpec(memory_space=pltpu.VMEM)
+    outs = pl.pallas_call(
+        functools.partial(attend_kernel, dims),
+        out_shape=jax.ShapeDtypeStruct((phases, nh, rows, GROUP * HEAD_DIM), jnp.bfloat16),
+        in_specs=[smem, smem, vmem, vmem, vmem],
+        out_specs=vmem,
+        compiler_params=pltpu.CompilerParams(vmem_limit_bytes=40 * 2**20),
+        name="attend_heads",
+    )(meta, order.astype(jnp.int32), visit_ids.reshape(-1, 128), qs, kv)
+    return pl.pallas_call(
+        functools.partial(exchange_kernel, dims),
+        out_shape=jax.ShapeDtypeStruct(queries.shape, jnp.bfloat16),
+        in_specs=[any_spec],
+        out_specs=any_spec,
+        scratch_shapes=[dma((phases,)), dma((phases, nh - 1)), dma((phases, nh - 1))],
+        compiler_params=pltpu.CompilerParams(collective_id=1, has_side_effects=True),
+        name="exchange_rows",
+    )(outs)
 
 
 def solution(mesh):

time: 81.5 us -> 109 us (1.34)
  the two profiles are of different devices: /device:TPU:0 before, /device:TPU:28 now
where the time goes in v3:
time: 109 us; the launch traced here: 111 us
  Pallas kernels  95 us (87%)
  local copies, waits for them, and re-layouts  7.55 us (7%)
  between operations  4.46 us (4%)
  other arithmetic  4.32 us (4%)
    pallas_call x1, Pallas kernels, fused_body(): pl.pallas_call(functools.partial(gather_kernel, dims), out_shape=(jax.Sha...  57 us
    pallas_call x1, Pallas kernels, fused_body(): pl.pallas_call(functools.partial(attend_kernel, dims), out_shape=jax.Shap...  24.3 us
    pallas_call x1, Pallas kernels, fused_body(): pl.pallas_call(functools.partial(exchange_kernel, dims), out_shape=jax.Sh...  13.7 us
    unnamed x9, local copies, waits for them, and re-layouts  7.55 us

profile of v3, /device:TPU:28, one launch (start us, length us, event | category | flops | bytes accessed | tf_op | source)
XLA Modules:
  0.0 111.3 jit_solution(8506233419293553485)
XLA Ops:
  0.0 1.4 %fusion = s32[]{:T(128)} fusion(s32[16]{0:T(128)} %param.9, s32[]{:T(128)S(6)} %axis_index.15), kind=kLoop, calls=%fused_computation.6 | loop fusion | flops 47 | bytes 72 | tf_op jit(solution)/shard_map/reduce_sum | solution.py:385
  2.1 0.8 select_reduce_fusion.order_ref
  2.8 1.4 %convert_reduce_fusion = (s32[]{:T(128)}, s32[]{:T(128)}, s32[]{:T(128)}) fusion(s32[3072]{0:T(1024)} %param.8), kind=kLoop, calls=%fused_computation | loop fusion | flops 27645 | bytes 12300 | tf_op jit(solution)/shard_map/reduce_sum | solution.py:386
  8.0 0.8 pad_add_fusion.meta_ref
  8.7 57.0 %gather_heads.1 = (bf16[4,2,3072,128]{3,2,1,0:T(8,128)(2,1)}, bf16[4,2,96,512]{3,2,1,0:T(8,128)(2,1)}) custom-call(bf16[96,4096]{1,0:T(8,128)(2,1)} %q_ref.1, bf16[96,1024]{1,0:T(8,128)(2,1)} %k_ref.1, bf16[96,1024]{1,0:T(8,128)(2,1)} %v_ref.1), custom_call_target="tpu_custom_call" | custom-call | tf_op jit(solution)/shard_map/gather_heads/pallas_call | solution.py:361
  65.7 0.0 copy-start
  65.7 2.8 %copy-done = bf16[4,2,3072,128]{3,2,1,0:T(8,128)(2,1)S(1)} copy-done((bf16[4,2,3072,128]{3,2,1,0:T(8,128)(2,1)S(1)}, bf16[4,2,3072,128]{3,2,1,0:T(8,128)(2,1)}, u32[]{:S(2)}) %copy-start) | copy-done | bytes 6291480
  68.5 0.0 copy-start.2
  68.5 1.1 %copy-done.2 = bf16[4,2,96,512]{3,2,1,0:T(8,128)(2,1)S(1)} copy-done((bf16[4,2,96,512]{3,2,1,0:T(8,128)(2,1)S(1)}, bf16[4,2,96,512]{3,2,1,0:T(8,128)(2,1)}, u32[]{:S(2)}) %copy-start.2) | copy-done | bytes 786456
  69.6 0.0 copy-start.3
  69.6 0.7 copy-done.3
  70.3 24.3 %attend_heads.1.outs = bf16[4,2,96,512]{3,2,1,0:T(8,128)(2,1)S(1)} custom-call(s32[2]{0:T(128)S(1)} %pad_add_fusion.meta_ref, s32[16]{0:T(128)S(1)} %select_reduce_fusion.order_ref, s32[24,128]{1,0:T(8,128)S(1)} %bitcast.3, bf16[4,2,96,512]{3,2,1,0:T(8,128)(2,1)S(1)} %copy-done.2, bf16[4,2,3072,128]{3,2,1,0:T(8,128)(2,1)S(1)} %copy-done), custom_call_target="tpu_custom_call" | custom-call | tf_op jit(solution)/shard_map/attend_heads/pallas_call | solution.py:393
  94.7 0.0 copy-start.1
  94.7 0.9 copy-done.1
  95.6 13.7 %exchange_rows.1 = bf16[96,4096]{1,0:T(8,128)(2,1)} custom-call(bf16[4,2,96,512]{3,2,1,0:T(8,128)(2,1)} %copy-done.1), custom_call_target="tpu_custom_call" | custom-call | tf_op jit(solution)/shard_map/exchange_rows/pallas_call | solution.py:401
  109.3 2.1 %copy.7 = bf16[96,4096]{1,0:T(8,128)(2,1)} copy(bf16[96,4096]{1,0:T(8,128)(2,1)} %exchange_rows.1) | data formatting | bytes 1572864
Async XLA Ops:
  65.7 2.8 %copy-start = (bf16[4,2,3072,128]{3,2,1,0:T(8,128)(2,1)S(1)}, bf16[4,2,3072,128]{3,2,1,0:T(8,128)(2,1)}, u32[]{:S(2)}) copy-start(bf16[4,2,3072,128]{3,2,1,0:T(8,128)(2,1)} %get-tuple-element.8.kv) | copy-start | bytes 18874372
  68.5 1.1 %copy-start.2 = (bf16[4,2,96,512]{3,2,1,0:T(8,128)(2,1)S(1)}, bf16[4,2,96,512]{3,2,1,0:T(8,128)(2,1)}, u32[]{:S(2)}) copy-start(bf16[4,2,96,512]{3,2,1,0:T(8,128)(2,1)} %get-tuple-element.7.qs) | copy-start | bytes 2359300
  69.6 0.7 copy-start.3
  94.7 0.9 copy-start.1

commit v4 on v2

--- a/solution.py
+++ b/solution.py
@@ -12,7 +12,6 @@
 HEAD_DIM = 128
 VISITS = 4
 GROUP = HEADS // KV_HEADS
-LOG2E = 1.4426950408889634
 
 MESH = pl.DeviceIdType.MESH
 
@@ -224,22 +223,27 @@
         for copy in own_copies(p):
             copy.start()
 
-    query_pos = span_ref[me] * block + lax.broadcasted_iota(jnp.int32, (block, 1), 0)
-    first = jnp.zeros((block, 1), jnp.int32)
+    columns = GROUP * block
+    column = lax.broadcasted_iota(jnp.int32, (1, columns), 1)
+    offset = column
+    for g in range(1, GROUP):
+        offset = jnp.where(column >= g * block, column - g * block, offset)
+    query_pos = span_ref[me] * block + offset
+    first = jnp.zeros((1, columns), jnp.int32)
     visits = visit_ref[...]
     for visit in range(1, VISITS):
         begin = jnp.sum(jnp.where(visits < visit, 1.0, 0.0), axis=1, keepdims=True)
         begin = jnp.sum(begin, axis=0, keepdims=True).astype(jnp.int32)
         first = jnp.where(begin <= query_pos, jnp.maximum(first, begin), first)
-    lane = lax.broadcasted_iota(jnp.int32, (1, 2 * block), 1)
-    for pair in range(nblk // 2):
-        key_pos = jnp.where(
-            lane < block,
-            span_ref[2 * pair] * block + lane,
-            span_ref[2 * pair + 1] * block + (lane - block),
-        )
+    row = lax.broadcasted_iota(jnp.int32, (block, 1), 0)
+
+    def mask_block(blk, carry):
+        key_pos = span_ref[blk] * block + row
         allowed = (key_pos <= query_pos) & (key_pos >= first)
-        bias[:, 2 * block * pair : 2 * block * (pair + 1)] = jnp.where(allowed, 0.0, -jnp.inf)
+        bias[pl.ds(pl.multiple_of(blk * block, 16), block), :] = jnp.where(allowed, 0.0, -jnp.inf)
+        return carry
+
+    lax.fori_loop(0, nblk, mask_block, 0)
 
     pl.semaphore_wait(barrier, nz + 1 + nh - 1)
 
@@ -251,8 +255,8 @@
             copy.start()
 
     chunk = next(size for size in (512, 384, 256, 128) if keys % size == 0)
-    batch = 2
-    scale = HEAD_DIM**-0.5 * LOG2E
+    batch = GROUP
+    scale = HEAD_DIM**-0.5
     lowest = -3.0e38
 
     def compute(p, part, events):
@@ -272,28 +276,27 @@
             start = pl.multiple_of(index * chunk, chunk)
             key = kv[p, 0, pl.ds(start, chunk), :]
             value = kv[p, 1, pl.ds(start, chunk), :]
-            extended = jnp.concatenate([value, jnp.ones_like(value)], axis=1)
+            extended = jnp.concatenate(
+                [jnp.transpose(value), jnp.ones((16, chunk), jnp.bfloat16)], axis=0
+            )
             score = lax.dot_general(
-                query, key, (((1,), (1,)), ((), ())), preferred_element_type=jnp.float32
+                key, query, (((1,), (1,)), ((), ())), preferred_element_type=jnp.float32
             )
-            mask = bias[:, pl.ds(start, chunk)]
-            shifted = jnp.concatenate(
-                [score[i * block : (i + 1) * block] * scale + mask for i in range(batch)], axis=0
-            )
-            new_max = jnp.maximum(run_max, jnp.max(shifted, axis=1, keepdims=True))
-            weight = jnp.exp2(shifted - new_max).astype(jnp.bfloat16)
-            factor = jnp.exp2(run_max - new_max)
+            shifted = score * scale + bias[pl.ds(start, chunk), :]
+            new_max = jnp.maximum(run_max, jnp.max(shifted, axis=0, keepdims=True))
+            weight = jnp.exp(shifted - new_max).astype(jnp.bfloat16)
+            factor = jnp.exp(run_max - new_max)
             new_acc = run_acc * factor + jnp.dot(
-                weight, extended, preferred_element_type=jnp.float32
+                extended, weight, preferred_element_type=jnp.float32
             )
             return new_max, new_acc
 
         initial = (
-            jnp.full((batch * block, 1), lowest, jnp.float32),
-            jnp.zeros((batch * block, 2 * HEAD_DIM), jnp.float32),
+            jnp.full((1, columns), lowest, jnp.float32),
+            jnp.zeros((HEAD_DIM + 16, columns), jnp.float32),
         )
         _, acc = lax.fori_loop(0, keys // chunk, step, initial)
-        result = (acc[:, :HEAD_DIM] / acc[:, HEAD_DIM:]).astype(jnp.bfloat16)
+        result = jnp.transpose(acc[:HEAD_DIM] / acc[HEAD_DIM : HEAD_DIM + 1]).astype(jnp.bfloat16)
         for i in range(batch):
             for h in range(nh):
                 first_row = i * block + h * rows
@@ -383,7 +386,7 @@
             pltpu.VMEM((phases, 2, nblk * block, HEAD_DIM), jnp.bfloat16),
             pltpu.VMEM((phases, nh, rows, GROUP * HEAD_DIM), jnp.bfloat16),
             pltpu.VMEM((phases, nh, rows, GROUP * HEAD_DIM), jnp.bfloat16),
-            pltpu.VMEM((block, nblk * block), jnp.float32),
+            pltpu.VMEM((nblk * block, GROUP * block), jnp.float32),
             dma((phases, nblk)),
             dma((phases, nz)),
             dma((phases, 2 * nz)),

time: 81.5 us -> 74.1 us (0.909)
  the two profiles are of different devices: /device:TPU:0 before, /device:TPU:12 now
where the time goes in v4:
time: 74.1 us; the launch traced here: 73.9 us
  Pallas kernels  71.8 us (97%)
  local copies, waits for them, and re-layouts  2.06 us (3%)
    pallas_call x1, Pallas kernels, fused_body(): pl.pallas_call(functools.partial(fused_kernel, (nz, nh, rows, phases)), o...  71.8 us
    unnamed x1, local copies, waits for them, and re-layouts  2.06 us

profile of v4, /device:TPU:12, one launch (start us, length us, event | category | flops | bytes accessed | tf_op | source)
XLA Modules:
  0.0 73.9 jit_solution(8482262968775312024)
XLA Ops:
  0.0 71.8 %visit_attention.1 = bf16[96,4096]{1,0:T(8,128)(2,1)} custom-call(bf16[96,4096]{1,0:T(8,128)(2,1)} %q_ref.1, bf16[96,1024]{1,0:T(8,128)(2,1)} %k_ref.1, bf16[96,1024]{1,0:T(8,128)(2,1)} %v_ref.1, s32[24,128]{1,0:T(8,128)} %bitcast.1, s32[16]{0:T(128)} %span_ref.1), custom_call_target="tpu_custom_call" | custom-call | tf_op jit(solution)/shard_map/visit_attention/pallas_call | solution.py:374
  71.8 2.1 %copy.7 = bf16[96,4096]{1,0:T(8,128)(2,1)} copy(bf16[96,4096]{1,0:T(8,128)(2,1)} %visit_attention.1) | data formatting | bytes 1572864

commit v5 on v4

--- a/solution.py
+++ b/solution.py
@@ -98,7 +98,7 @@
 def fused_kernel(
     dims, q_ref, k_ref, v_ref, visit_ref, span_ref, out_ref,
     kv, qs, outs, bias,
-    kv_recv, y_send, core_send, z_send, x_send, x_recv, own_sem, out_send, out_recv, out_own,
+    kv_recv, side_recv, y_send, core_send, z_send, side_send, x_send, x_recv, own_sem, out_send, out_recv, out_own,
 ):
     nz, nh, rows, phases = dims
     nblk = 4 * nz
@@ -111,17 +111,28 @@
     def index_of(z_at, y_at, core_at):
         return z_at * 4 + y_at * 2 + core_at
 
-    z_peers = [lax.rem(z + step, nz) for step in range(1, nz)]
-    z_ids = [index_of(zp, y, core) for zp in z_peers]
     y_id = index_of(z, 1 - y, core)
     core_id = index_of(z, y, 1 - core)
     x_peers = [lax.rem(x + step, nh) for step in range(1, nh)]
+    side_rows = max(16, block // (2 * (nz - 1)) // 16 * 16)
+
+    def next_plane(up):
+        return z + 1 if up else z - 1
+
+    def has_next(up):
+        return z + 1 < nz if up else z > 0
 
     barrier = pltpu.get_barrier_semaphore()
-    for blk in z_ids + [y_id, core_id]:
+    for blk in (y_id, core_id):
         pl.semaphore_signal(barrier, inc=1, device_id=(blk, x), device_id_type=MESH)
     for xp in x_peers:
         pl.semaphore_signal(barrier, inc=1, device_id=(me, xp), device_id_type=MESH)
+    for up in (True, False):
+
+        @pl.when(has_next(up))
+        def _(up=up):
+            target = index_of(next_plane(up), y, core)
+            pl.semaphore_signal(barrier, inc=1, device_id=(target, x), device_id_type=MESH)
 
     def sources(p, to):
         kv_at = pl.multiple_of((to * phases + p) * HEAD_DIM, HEAD_DIM)
@@ -161,63 +172,116 @@
                 )
         return result
 
-    def block_ref(p, blk):
-        return kv.at[p, :, pl.ds(pl.multiple_of(blk * block, 16), block), :]
-
-    def gather_copy(p, blk, send_sem, target):
+    def rows_ref(p, blk, first_row, count):
+        at = pl.multiple_of(blk * block + first_row, 16)
+        return kv.at[p, :, pl.ds(at, count), :]
+
+    def remote(ref, send_sem, recv_sem, target):
         return pltpu.make_async_remote_copy(
-            src_ref=block_ref(p, blk), dst_ref=block_ref(p, blk),
-            send_sem=send_sem, recv_sem=kv_recv.at[p, blk],
+            src_ref=ref, dst_ref=ref, send_sem=send_sem, recv_sem=recv_sem,
             device_id=(target, x), device_id_type=MESH,
         )
 
-    def await_block(p, blk):
-        gather_copy(p, blk, y_send.at[p, 0], y_id).wait_recv()
-
-    def own_sends(p):
-        copies = [gather_copy(p, me, y_send.at[p, 0], y_id)]
-        for step, blk in enumerate(z_ids):
-            copies.append(gather_copy(p, me, z_send.at[p, step], blk))
-        copies.append(gather_copy(p, me, core_send.at[p, 0], core_id))
-        return copies
+    def whole_copy(p, blk, send_sem, target):
+        return remote(rows_ref(p, blk, 0, block), send_sem, kv_recv.at[p, blk], target)
+
+    def y_copy(p, plane):
+        blk = index_of(plane, y, core)
+        if plane is z:
+            return whole_copy(p, blk, y_send.at[p, plane], y_id)
+        ref = rows_ref(p, blk, side_rows, block - side_rows)
+        return remote(ref, y_send.at[p, plane], kv_recv.at[p, blk], y_id)
+
+    def core_copy(p, plane, side):
+        blk = index_of(plane, y if side == 0 else 1 - y, core)
+        return whole_copy(p, blk, core_send.at[p, side, plane], core_id)
+
+    def z_copy(p, plane, up):
+        blk, to = index_of(plane, y, core), index_of(next_plane(up), y, core)
+        return whole_copy(p, blk, z_send.at[p, int(up), plane], to)
+
+    def side_copy(p, plane, up):
+        blk, to = index_of(plane, 1 - y, core), index_of(next_plane(up), y, core)
+        ref = rows_ref(p, blk, 0, side_rows)
+        return remote(ref, side_send.at[p, int(up), plane], side_recv.at[p, plane], to)
+
+    def await_whole(p, blk):
+        whole_copy(p, blk, y_send.at[p, 0], y_id).wait_recv()
+
+    def for_next(make, act):
+        for up in (True, False):
+            pl.when(has_next(up))(functools.partial(lambda up: act(make(up)), up))
+
+    def start(copy):
+        copy.start()
+
+    def finish(copy):
+        copy.wait_send()
 
     def start_own(p):
         for copy in own_copies(p, 2):
             copy.wait()
         for copy in x_copies(p, (0, 1)):
             copy.wait()
-        for copy in own_sends(p):
-            copy.start()
-
-    def z_block(step):
-        return index_of(lax.rem(z + nz - 1 - step, nz), y, core)
-
-    def z_forwards(p, step):
-        blk = z_block(step)
-        return [
-            gather_copy(p, blk, y_send.at[p, 1 + step], y_id),
-            gather_copy(p, blk, core_send.at[p, 1 + step], core_id),
-        ]
-
-    def forward_z(p, step):
-        await_block(p, z_block(step))
-        for copy in z_forwards(p, step):
-            copy.start()
-
-    def y_block(step):
-        return index_of(lax.rem(z + nz - step, nz), 1 - y, core)
-
-    def y_forward(p, step):
-        return gather_copy(p, y_block(step), core_send.at[p, nz + step], core_id)
-
-    def forward_y(p, step):
-        await_block(p, y_block(step))
-        y_forward(p, step).start()
-
-    def await_core(p):
-        for side in (y, 1 - y):
-            for step in range(nz):
-                await_block(p, index_of(lax.rem(z + nz - step, nz), side, 1 - core))
+        y_copy(p, z).start()
+        for_next(lambda up: z_copy(p, z, up), start)
+        core_copy(p, z, 0).start()
+
+    def pass_peer(p):
+        await_whole(p, index_of(z, 1 - y, core))
+        for_next(lambda up: side_copy(p, z, up), start)
+        core_copy(p, z, 1).start()
+
+    def from_planes(distance, act):
+        for up in (True, False):
+            plane = z - distance if up else z + distance
+            exists = plane >= 0 if up else plane < nz
+            pl.when(exists)(functools.partial(act, plane, up))
+
+    def pass_plane(p, distance):
+        def act(plane, up):
+            await_whole(p, index_of(plane, y, core))
+
+            @pl.when(has_next(up))
+            def _():
+                z_copy(p, plane, up).start()
+
+            y_copy(p, plane).start()
+            core_copy(p, plane, 0).start()
+            remote(
+                rows_ref(p, index_of(plane, 1 - y, core), 0, side_rows),
+                side_send.at[p, 0, 0], side_recv.at[p, plane], y_id,
+            ).wait_recv()
+
+            @pl.when(has_next(up))
+            def _():
+                side_copy(p, plane, up).start()
+
+        from_planes(distance, act)
+
+    def finish_plane(p, distance):
+        def act(plane, up):
+            @pl.when(has_next(up))
+            def _():
+                z_copy(p, plane, up).wait_send()
+                side_copy(p, plane, up).wait_send()
+
+            y_copy(p, plane).wait_send()
+            core_copy(p, plane, 0).wait_send()
+
+        from_planes(distance, act)
+
+    def plane_at(rank):
+        return lax.rem(z + jnp.where(2 * z < nz, rank, nz - rank), nz)
+
+    def pass_far(p, rank):
+        plane = plane_at(rank)
+        blk = index_of(plane, 1 - y, core)
+        remote(
+            rows_ref(p, blk, side_rows, block - side_rows),
+            y_send.at[p, 0], kv_recv.at[p, blk], y_id,
+        ).wait_recv()
+        core_copy(p, plane, 1).start()
 
     for p in range(phases):
         for copy in own_copies(p):
@@ -245,22 +309,20 @@
 
     lax.fori_loop(0, nblk, mask_block, 0)
 
-    pl.semaphore_wait(barrier, nz + 1 + nh - 1)
-
-    for p in range(phases):
-        for copy in x_copies(p, (0, 1)):
+    planes_beside = jnp.minimum(z, 1) + jnp.minimum(nz - 1 - z, 1)
+    pl.semaphore_wait(barrier, 1 + nh + planes_beside)
+
+    def start_x(p, kinds):
+        for copy in x_copies(p, kinds):
             copy.start()
-    for p in range(phases):
-        for copy in x_copies(p, (2,)):
-            copy.start()
-
-    chunk = next(size for size in (512, 384, 256, 128) if keys % size == 0)
+
+    chunk = 2 * block
     batch = GROUP
     scale = HEAD_DIM**-0.5
     lowest = -3.0e38
 
-    def compute(p, part, events):
-        at = part * batch
+    def compute(p, events):
+        at = 0
         query = jnp.concatenate(
             [
                 jnp.concatenate([qs[p, h, :, g * HEAD_DIM : (g + 1) * HEAD_DIM] for h in range(nh)], axis=0)
@@ -273,7 +335,10 @@
             for slot, event in events:
                 pl.when(index == slot)(event)
             run_max, run_acc = state
-            start = pl.multiple_of(index * chunk, chunk)
+            plane = plane_at(lax.rem(index, nz))
+            chip = plane * 2 + jnp.where(index < nz, y, 1 - y)
+            await_whole(p, chip * 2 + 1 - core)
+            start = pl.multiple_of(chip * chunk, 128)
             key = kv[p, 0, pl.ds(start, chunk), :]
             value = kv[p, 1, pl.ds(start, chunk), :]
             extended = jnp.concatenate(
@@ -295,7 +360,7 @@
             jnp.full((1, columns), lowest, jnp.float32),
             jnp.zeros((HEAD_DIM + 16, columns), jnp.float32),
         )
-        _, acc = lax.fori_loop(0, keys // chunk, step, initial)
+        _, acc = lax.fori_loop(0, 2 * nz, step, initial)
         result = jnp.transpose(acc[:HEAD_DIM] / acc[HEAD_DIM : HEAD_DIM + 1]).astype(jnp.bfloat16)
         for i in range(batch):
             for h in range(nh):
@@ -304,64 +369,67 @@
                     first_row : first_row + rows
                 ]
 
-    width = batch * HEAD_DIM
-    parts = GROUP // batch
-
-    def out_copies(p, part):
-        at = pl.multiple_of(((x * phases + p) * parts + part) * width, width)
-        place = out_ref.at[:, pl.ds(at, width)]
-        held = pl.ds(part * width, width)
-        copies = [pltpu.make_async_copy(outs.at[p, x, :, held], place, out_own.at[p, part])]
+    width = GROUP * HEAD_DIM
+
+    def out_copies(p):
+        place = out_ref.at[:, pl.ds(pl.multiple_of((x * phases + p) * width, width), width)]
+        copies = [pltpu.make_async_copy(outs.at[p, x], place, out_own.at[p])]
         for step, xp in enumerate(x_peers):
             copies.append(
                 pltpu.make_async_remote_copy(
-                    src_ref=outs.at[p, xp, :, held], dst_ref=place,
-                    send_sem=out_send.at[p, part, step], recv_sem=out_recv.at[p, part, step],
+                    src_ref=outs.at[p, xp], dst_ref=place,
+                    send_sem=out_send.at[p, step], recv_sem=out_recv.at[p, step],
                     device_id=(me, xp), device_id_type=MESH,
                 )
             )
         return copies
 
-    chunks = keys // chunk
-    slots = chunks * parts
-
     def events_of(p):
-        events = [functools.partial(forward_y, p, 0)]
-        events += [functools.partial(forward_z, p, step) for step in range(nz - 1)]
-        return [(min(slots - 1, (k + 1) * slots // (len(events) + 1)), e) for k, e in enumerate(events)]
-
-    for p in range(min(2, phases)):
+        events = []
+        for rank in range(1, nz):
+            events.append((2 * rank, functools.partial(pass_far, p, rank)))
+        if p + 1 < phases:
+            events.append((0, functools.partial(pass_peer, p + 1)))
+            for distance in range(1, nz):
+                events.append((2 * distance - 1, functools.partial(pass_plane, p + 1, distance)))
+        return events
+
+    start_x(0, (0, 1))
+    start_own(0)
+    for p in range(1, min(2, phases)):
+        start_x(p, (0, 1))
+        start_x(p - 1, (2,))
         start_own(p)
-    for step in range(nz - 1):
-        forward_z(0, step)
-    forward_y(0, 0)
+    pass_peer(0)
+    for p in range(min(2, phases), min(3, phases)):
+        start_x(p, (0, 1))
+    start_x(min(2, phases) - 1, (2,))
+    for distance in range(1, nz):
+        pass_plane(0, distance)
     for p in range(phases):
         if p + 2 < phases:
             start_own(p + 2)
-        for step in range(1, nz):
-            forward_y(p, step)
+            start_x(p + 2, (2,))
+            if p + 3 < phases:
+                start_x(p + 3, (0, 1))
         for copy in own_copies(p, 3, 2):
             copy.wait()
         for copy in x_copies(p, (2,)):
             copy.wait()
-        await_core(p)
-        events = events_of(p + 1) if p + 1 < phases else []
-        for part in range(parts):
-            low = part * chunks
-            compute(p, part, [(slot - low, e) for slot, e in events if low <= slot < low + chunks])
-            for copy in out_copies(p, part):
-                copy.start()
+        compute(p, events_of(p))
+        for copy in out_copies(p):
+            copy.start()
     for p in range(phases):
-        for part in range(parts):
-            for copy in out_copies(p, part):
-                copy.wait()
-        for copy in own_sends(p):
-            copy.wait_send()
-        for step in range(nz - 1):
-            for copy in z_forwards(p, step):
-                copy.wait_send()
-        for step in range(nz):
-            y_forward(p, step).wait_send()
+        for copy in out_copies(p):
+            copy.wait()
+        y_copy(p, z).wait_send()
+        for_next(lambda up: z_copy(p, z, up), finish)
+        for_next(lambda up: side_copy(p, z, up), finish)
+        for side in range(2):
+            core_copy(p, z, side).wait_send()
+        for distance in range(1, nz):
+            finish_plane(p, distance)
+            core_copy(p, plane_at(distance), 1).wait_send()
 
 
 def fused_body(nblk, nh, queries, key_rows, value_rows, visit_ids, span_order):
@@ -381,7 +449,7 @@
             pl.BlockSpec(memory_space=pltpu.VMEM),
             pl.BlockSpec(memory_space=pltpu.SMEM),
         ],
-        out_specs=pl.BlockSpec(memory_space=pltpu.VMEM),
+        out_specs=any_spec,
         scratch_shapes=[
             pltpu.VMEM((phases, 2, nblk * block, HEAD_DIM), jnp.bfloat16),
             pltpu.VMEM((phases, nh, rows, GROUP * HEAD_DIM), jnp.bfloat16),
@@ -389,14 +457,16 @@
             pltpu.VMEM((nblk * block, GROUP * block), jnp.float32),
             dma((phases, nblk)),
             dma((phases, nz)),
-            dma((phases, 2 * nz)),
-            dma((phases, nz - 1)),
+            dma((phases, nz)),
+            dma((phases, 2, nz)),
+            dma((phases, 2, nz)),
+            dma((phases, 2, nz)),
             dma((phases, nh - 1, 3)),
             dma((phases, nh - 1, 3)),
             dma((phases, 3)),
-            dma((phases, GROUP, nh - 1)),
-            dma((phases, GROUP, nh - 1)),
-            dma((phases, GROUP)),
+            dma((phases, nh - 1)),
+            dma((phases, nh - 1)),
+            dma((phases,)),
         ],
         compiler_params=pltpu.CompilerParams(
             collective_id=0, has_side_effects=True, vmem_limit_bytes=60 * 2**20

time: 74.1 us -> 75.9 us (1.024)
  the two profiles are of different devices: /device:TPU:12 before, /device:TPU:0 now
where the time goes in v5:
time: 75.9 us; the launch traced here: 75.6 us
  Pallas kernels  73.6 us (97%)
  local copies, waits for them, and re-layouts  2.06 us (3%)
    pallas_call x1, Pallas kernels, fused_body(): pl.pallas_call(functools.partial(fused_kernel, (nz, nh, rows, phases)), o...  73.6 us
    unnamed x1, local copies, waits for them, and re-layouts  2.06 us

profile of v5, /device:TPU:0, one launch (start us, length us, event | category | flops | bytes accessed | tf_op | source)
XLA Modules:
  0.0 75.6 jit_solution(10397508631996284227)
XLA Ops:
  0.0 73.6 %visit_attention.1 = bf16[96,4096]{1,0:T(8,128)(2,1)} custom-call(bf16[96,4096]{1,0:T(8,128)(2,1)} %q_ref.1, bf16[96,1024]{1,0:T(8,128)(2,1)} %k_ref.1, bf16[96,1024]{1,0:T(8,128)(2,1)} %v_ref.1, s32[24,128]{1,0:T(8,128)} %bitcast.1, s32[16]{0:T(128)} %span_ref.1), custom_call_target="tpu_custom_call" | custom-call | tf_op jit(solution)/shard_map/visit_attention/pallas_call | solution.py:442
  73.6 2.1 %copy.7 = bf16[96,4096]{1,0:T(8,128)(2,1)} copy(bf16[96,4096]{1,0:T(8,128)(2,1)} %visit_attention.1) | data formatting | bytes 1572864

commit v6 on v5

--- a/solution.py
+++ b/solution.py
@@ -12,6 +12,7 @@
 HEAD_DIM = 128
 VISITS = 4
 GROUP = HEADS // KV_HEADS
+LOG2E = 1.4426950408889634
 
 MESH = pl.DeviceIdType.MESH
 
@@ -318,7 +319,7 @@
 
     chunk = 2 * block
     batch = GROUP
-    scale = HEAD_DIM**-0.5
+    scale = HEAD_DIM**-0.5 * LOG2E
     lowest = -3.0e38
 
     def compute(p, events):
@@ -331,26 +332,29 @@
             axis=0,
         )
 
+        query_t = jnp.transpose(query)
+
         def step(index, state):
             for slot, event in events:
                 pl.when(index == slot)(event)
             run_max, run_acc = state
-            plane = plane_at(lax.rem(index, nz))
-            chip = plane * 2 + jnp.where(index < nz, y, 1 - y)
-            await_whole(p, chip * 2 + 1 - core)
-            start = pl.multiple_of(chip * chunk, 128)
-            key = kv[p, 0, pl.ds(start, chunk), :]
-            value = kv[p, 1, pl.ds(start, chunk), :]
+            starts = []
+            for rank in (2 * index, 2 * index + 1):
+                plane = plane_at(lax.rem(rank, nz))
+                chip = plane * 2 + jnp.where(rank < nz, y, 1 - y)
+                await_whole(p, chip * 2 + 1 - core)
+                starts.append(pl.multiple_of(chip * chunk, 128))
+            key = jnp.concatenate([kv[p, 0, pl.ds(at, chunk), :] for at in starts], axis=0)
+            value = jnp.concatenate([kv[p, 1, pl.ds(at, chunk), :] for at in starts], axis=0)
+            mask = jnp.concatenate([bias[pl.ds(at, chunk), :] for at in starts], axis=0)
             extended = jnp.concatenate(
-                [jnp.transpose(value), jnp.ones((16, chunk), jnp.bfloat16)], axis=0
+                [jnp.transpose(value), jnp.ones((16, 2 * chunk), jnp.bfloat16)], axis=0
             )
-            score = lax.dot_general(
-                key, query, (((1,), (1,)), ((), ())), preferred_element_type=jnp.float32
-            )
-            shifted = score * scale + bias[pl.ds(start, chunk), :]
+            score = jnp.dot(key, query_t, preferred_element_type=jnp.float32)
+            shifted = score * scale + mask
             new_max = jnp.maximum(run_max, jnp.max(shifted, axis=0, keepdims=True))
-            weight = jnp.exp(shifted - new_max).astype(jnp.bfloat16)
-            factor = jnp.exp(run_max - new_max)
+            weight = jnp.exp2(shifted - new_max).astype(jnp.bfloat16)
+            factor = jnp.exp2(run_max - new_max)
             new_acc = run_acc * factor + jnp.dot(
                 extended, weight, preferred_element_type=jnp.float32
             )
@@ -360,7 +364,7 @@
             jnp.full((1, columns), lowest, jnp.float32),
             jnp.zeros((HEAD_DIM + 16, columns), jnp.float32),
         )
-        _, acc = lax.fori_loop(0, 2 * nz, step, initial)
+        _, acc = lax.fori_loop(0, nz, step, initial)
         result = jnp.transpose(acc[:HEAD_DIM] / acc[HEAD_DIM : HEAD_DIM + 1]).astype(jnp.bfloat16)
         for i in range(batch):
             for h in range(nh):
@@ -387,11 +391,11 @@
     def events_of(p):
         events = []
         for rank in range(1, nz):
-            events.append((2 * rank, functools.partial(pass_far, p, rank)))
+            events.append((min(rank, nz - 2), functools.partial(pass_far, p, rank)))
         if p + 1 < phases:
             events.append((0, functools.partial(pass_peer, p + 1)))
             for distance in range(1, nz):
-                events.append((2 * distance - 1, functools.partial(pass_plane, p + 1, distance)))
+                events.append((distance, functools.partial(pass_plane, p + 1, distance)))
         return events
 
     start_x(0, (0, 1))
@@ -486,7 +490,7 @@
     nblk, nh = mesh.shape["blk"], mesh.shape["head"]
 
     def body(queries, *rest):
-        if queries.shape[0] % 16 == 0 and nblk % 4 == 0 and KV_HEADS % nh == 0:
+        if queries.shape[0] % 16 == 0 and nblk % 8 == 0 and KV_HEADS % nh == 0:
             return fused_body(nblk, nh, queries, *rest)
         return gathered_body(queries, *rest)
 

time: 75.9 us -> 67.5 us (0.89)
  Pallas kernels: 73.6 us -> 65.2 us
    pallas_call x1, Pallas kernels: 73.6 us -> 65.2 us  [fused_body(): pl.pallas_call(functools.partial(fused_kernel, (nz, nh, rows, phases)), o...]
where the time goes in v6:
time: 67.5 us; the launch traced here: 67.3 us
  Pallas kernels  65.2 us (97%)
  local copies, waits for them, and re-layouts  2.06 us (3%)
    pallas_call x1, Pallas kernels, fused_body(): pl.pallas_call(functools.partial(fused_kernel, (nz, nh, rows, phases)), o...  65.2 us
    unnamed x1, local copies, waits for them, and re-layouts  2.06 us

profile of v6, /device:TPU:0, one launch (start us, length us, event | category | flops | bytes accessed | tf_op | source)
XLA Modules:
  0.0 67.3 jit_solution(1641536071114456670)
XLA Ops:
  0.0 65.2 %visit_attention.1 = bf16[96,4096]{1,0:T(8,128)(2,1)} custom-call(bf16[96,4096]{1,0:T(8,128)(2,1)} %q_ref.1, bf16[96,1024]{1,0:T(8,128)(2,1)} %k_ref.1, bf16[96,1024]{1,0:T(8,128)(2,1)} %v_ref.1, s32[24,128]{1,0:T(8,128)} %bitcast.1, s32[16]{0:T(128)} %span_ref.1), custom_call_target="tpu_custom_call" | custom-call | tf_op jit(solution)/shard_map/visit_attention/pallas_call | solution.py:446
  65.2 2.1 %copy.7 = bf16[96,4096]{1,0:T(8,128)(2,1)} copy(bf16[96,4096]{1,0:T(8,128)(2,1)} %visit_attention.1) | data formatting | bytes 1572864

commit v7 on v6

--- a/solution.py
+++ b/solution.py
@@ -307,8 +307,6 @@
         allowed = (key_pos <= query_pos) & (key_pos >= first)
         bias[pl.ds(pl.multiple_of(blk * block, 16), block), :] = jnp.where(allowed, 0.0, -jnp.inf)
         return carry
-
-    lax.fori_loop(0, nblk, mask_block, 0)
 
     planes_beside = jnp.minimum(z, 1) + jnp.minimum(nz - 1 - z, 1)
     pl.semaphore_wait(barrier, 1 + nh + planes_beside)
@@ -390,6 +388,8 @@
 
     def events_of(p):
         events = []
+        if p == 0:
+            events.append((nz // 2 - 1, functools.partial(pass_plane, 0, nz - 1)))
         for rank in range(1, nz):
             events.append((min(rank, nz - 2), functools.partial(pass_far, p, rank)))
         if p + 1 < phases:
@@ -399,17 +399,19 @@
         return events
 
     start_x(0, (0, 1))
+    lax.fori_loop(0, nblk, mask_block, 0)
     start_own(0)
-    for p in range(1, min(2, phases)):
-        start_x(p, (0, 1))
-        start_x(p - 1, (2,))
-        start_own(p)
+    if phases > 1:
+        start_x(1, (0, 1))
+    start_x(0, (2,))
     pass_peer(0)
-    for p in range(min(2, phases), min(3, phases)):
-        start_x(p, (0, 1))
-    start_x(min(2, phases) - 1, (2,))
-    for distance in range(1, nz):
+    for distance in range(1, nz - 1):
         pass_plane(0, distance)
+    if phases > 1:
+        start_own(1)
+        start_x(1, (2,))
+    if phases > 2:
+        start_x(2, (0, 1))
     for p in range(phases):
         if p + 2 < phases:
             start_own(p + 2)

time: 67.5 us -> 70.6 us (1.046)
  Pallas kernels: 65.2 us -> 68.3 us
    pallas_call x1, Pallas kernels: 65.2 us -> 68.3 us  [fused_body(): pl.pallas_call(functools.partial(fused_kernel, (nz, nh, rows, phases)), o...]
where the time goes in v7:
time: 70.6 us; the launch traced here: 70.3 us
  Pallas kernels  68.3 us (97%)
  local copies, waits for them, and re-layouts  2.06 us (3%)
    pallas_call x1, Pallas kernels, fused_body(): pl.pallas_call(functools.partial(fused_kernel, (nz, nh, rows, phases)), o...  68.3 us
    unnamed x1, local copies, waits for them, and re-layouts  2.06 us

profile of v7, /device:TPU:0, one launch (start us, length us, event | category | flops | bytes accessed | tf_op | source)
XLA Modules:
  0.0 70.3 jit_solution(10636286702239161989)
XLA Ops:
  0.0 68.3 %visit_attention.1 = bf16[96,4096]{1,0:T(8,128)(2,1)} custom-call(bf16[96,4096]{1,0:T(8,128)(2,1)} %q_ref.1, bf16[96,1024]{1,0:T(8,128)(2,1)} %k_ref.1, bf16[96,1024]{1,0:T(8,128)(2,1)} %v_ref.1, s32[24,128]{1,0:T(8,128)} %bitcast.1, s32[16]{0:T(128)} %span_ref.1), custom_call_target="tpu_custom_call" | custom-call | tf_op jit(solution)/shard_map/visit_attention/pallas_call | solution.py:448
  68.3 2.1 %copy.7 = bf16[96,4096]{1,0:T(8,128)(2,1)} copy(bf16[96,4096]{1,0:T(8,128)(2,1)} %visit_attention.1) | data formatting | bytes 1572864

commit v8 on v6

--- a/solution.py
+++ b/solution.py
@@ -307,8 +307,6 @@
         allowed = (key_pos <= query_pos) & (key_pos >= first)
         bias[pl.ds(pl.multiple_of(blk * block, 16), block), :] = jnp.where(allowed, 0.0, -jnp.inf)
         return carry
-
-    lax.fori_loop(0, nblk, mask_block, 0)
 
     planes_beside = jnp.minimum(z, 1) + jnp.minimum(nz - 1 - z, 1)
     pl.semaphore_wait(barrier, 1 + nh + planes_beside)
@@ -399,11 +397,12 @@
         return events
 
     start_x(0, (0, 1))
+    lax.fori_loop(0, nblk, mask_block, 0)
     start_own(0)
     for p in range(1, min(2, phases)):
         start_x(p, (0, 1))
+        start_own(p)
         start_x(p - 1, (2,))
-        start_own(p)
     pass_peer(0)
     for p in range(min(2, phases), min(3, phases)):
         start_x(p, (0, 1))

time: 67.5 us -> 67.6 us (level)
  no operation moved by 1% of the time
where the time goes in v8:
time: 67.6 us; the launch traced here: 67.4 us
  Pallas kernels  65.3 us (97%)
  local copies, waits for them, and re-layouts  2.06 us (3%)
    pallas_call x1, Pallas kernels, fused_body(): pl.pallas_call(functools.partial(fused_kernel, (nz, nh, rows, phases)), o...  65.3 us
    unnamed x1, local copies, waits for them, and re-layouts  2.06 us

profile of v8, /device:TPU:0, one launch (start us, length us, event | category | flops | bytes accessed | tf_op | source)
XLA Modules:
  0.0 67.4 jit_solution(16913857881089735728)
XLA Ops:
  0.0 65.3 %visit_attention.1 = bf16[96,4096]{1,0:T(8,128)(2,1)} custom-call(bf16[96,4096]{1,0:T(8,128)(2,1)} %q_ref.1, bf16[96,1024]{1,0:T(8,128)(2,1)} %k_ref.1, bf16[96,1024]{1,0:T(8,128)(2,1)} %v_ref.1, s32[24,128]{1,0:T(8,128)} %bitcast.1, s32[16]{0:T(128)} %span_ref.1), custom_call_target="tpu_custom_call" | custom-call | tf_op jit(solution)/shard_map/visit_attention/pallas_call | solution.py:445
  65.3 2.1 %copy.7 = bf16[96,4096]{1,0:T(8,128)(2,1)} copy(bf16[96,4096]{1,0:T(8,128)(2,1)} %visit_attention.1) | data formatting | bytes 1572864
